TPU v7x, 128 devices: a whole 4x4x4 slice. The times are simulated.
128 devices in a mesh: rep: 16 (over y_lo, z, core), tp: 8 (over y_hi, x).
Axes of the slice: x: 4, y: 4 (y_hi: 2, y_lo: 2; y = y_hi * 2 + y_lo), z: 4, core: 2. Of those that a mesh axis runs over, the one named last changes fastest.
Arguments:
- hidden: bfloat16 [2, 32, 8192], P(None, 'rep'), may hold values from -6 to 6
- queries: bfloat16 [2, 32, 8192], P(None, 'rep', 'tp'), may hold values from -160 to 160
- sectioned: bfloat16 [8192, 2048], P('rep', 'tp'), may hold values from -0.0625 to 0.0625
- owners: int32 [16], replicated, may hold values from 0 to 15, each once
- rotated_key_cache: bfloat16 [32, 8192, 1024], P('rep', None, 'tp'), may hold values from -6 to 6
- stored_value_cache: bfloat16 [32, 8192, 1024], P('rep', None, 'tp'), may hold values from -6 to 6
- lengths: int32 [32], P('rep'), may hold values from 2 to 8190, as said below
- out_weight: bfloat16 [8192, 4096], P('tp'), may hold values from -0.71875 to 0.71875
Outputs:
- installed: bfloat16 [8192, 2048], P(None, 'tp')
- appended: bfloat16 [2, 32, 2048], P(None, 'rep', 'tp')
- attention_out: bfloat16 [2, 32, 4096], P(None, 'rep')
Inputs may be any that keep to these rules, and one draw needn't show every extreme that they name: `lengths`: session 0 has the most filled slots.
All inputs are finite; a program needn't handle non-finite values.
Results may differ from a plain program's by a relative error of at most 0.0062.
Values may be sent and summed in bfloat16 or wider, within the bound.
A program may use at most 128 MiB of HBM per device.

v0:
```python
import jax
import jax.numpy as jnp
from jax import lax
from jax.sharding import PartitionSpec as P

HEAD_DIM = 128


rope_base = 500000.0


def rotate(vectors, positions):
    halfway = vectors.shape[-1] // 2
    frequency = jnp.exp(-jnp.log(rope_base) * jnp.arange(halfway, dtype=jnp.float32) / halfway)
    angles = positions.astype(jnp.float32)[..., None] * frequency
    first_part = vectors[..., :halfway]
    second_part = vectors[..., halfway:]
    return jnp.concatenate(
        [
            first_part * jnp.cos(angles) - second_part * jnp.sin(angles),
            second_part * jnp.cos(angles) + first_part * jnp.sin(angles),
        ],
        axis=-1,
    )


def shards(
    hidden, queries, sectioned, owners, rotated_key_cache, stored_value_cache, lengths, out_weight
):
    replicas = lax.axis_size("rep")
    block_rows = sectioned.shape[0]
    columns = sectioned.shape[1]
    step_count, sessions, model_width = hidden.shape
    flat_hidden = hidden.reshape(step_count * sessions, model_width)
    pooled = lax.all_gather(sectioned, "rep", axis=0, tiled=True)
    installed = jnp.take(pooled.reshape(replicas, block_rows, columns), owners, axis=0).reshape(
        replicas * block_rows, columns
    )
    projected_rows = jnp.dot(flat_hidden, installed, preferred_element_type=jnp.float32)
    local_heads = rotated_key_cache.shape[2] // HEAD_DIM
    group_size = queries.shape[2] // (local_heads * HEAD_DIM)
    cache_slots = rotated_key_cache.shape[1]
    score_scale = HEAD_DIM ** (-0.5)
    query_head_rows = queries.reshape(step_count, sessions, local_heads, group_size, HEAD_DIM)
    stored_keys = rotated_key_cache.reshape(sessions, cache_slots, local_heads, HEAD_DIM)
    stored_values = stored_value_cache.reshape(sessions, cache_slots, local_heads, HEAD_DIM)
    scores_cache = (
        jnp.einsum(
            "tsgqd,scgd->tsgqc", query_head_rows, stored_keys, preferred_element_type=jnp.float32
        )
        * score_scale
    )
    valid_slots = lax.broadcasted_iota(jnp.int32, (sessions, cache_slots), 1) < lengths[:, None]
    scores_cache = jnp.where(valid_slots[None, :, None, None, :], scores_cache, -jnp.inf)
    projected_rows = projected_rows.reshape(step_count, sessions, local_heads, 2, HEAD_DIM)
    positions = lengths[None, :] + lax.broadcasted_iota(jnp.int32, (step_count, sessions), 0)
    incoming_keys = rotate(projected_rows[:, :, :, 0], positions[:, :, None]).astype(jnp.bfloat16)
    incoming_values = projected_rows[:, :, :, 1].astype(jnp.bfloat16)
    appended = jnp.stack([incoming_keys, incoming_values], axis=3).reshape(
        step_count, sessions, local_heads * 2 * HEAD_DIM
    )
    scores_new = (
        jnp.einsum(
            "tsgqd,usgd->tsgqu", query_head_rows, incoming_keys, preferred_element_type=jnp.float32
        )
        * score_scale
    )
    causal_mask = lax.broadcasted_iota(
        jnp.int32, (step_count, step_count), 1
    ) <= lax.broadcasted_iota(jnp.int32, (step_count, step_count), 0)
    scores_new = jnp.where(causal_mask[:, None, None, None, :], scores_new, -jnp.inf)
    largest = jnp.maximum(jnp.max(scores_cache, axis=-1), jnp.max(scores_new, axis=-1))
    exp_cache = jnp.exp(scores_cache - largest[..., None])
    exp_new = jnp.exp(scores_new - largest[..., None])
    totals = jnp.sum(exp_cache, axis=-1) + jnp.sum(exp_new, axis=-1)
    weights_cache = (exp_cache / totals[..., None]).astype(jnp.bfloat16)
    weights_new = (exp_new / totals[..., None]).astype(jnp.bfloat16)
    attended = jnp.einsum(
        "tsgqc,scgd->tsgqd", weights_cache, stored_values, preferred_element_type=jnp.float32
    )
    attended = attended + jnp.einsum(
        "tsgqu,usgd->tsgqd", weights_new, incoming_values, preferred_element_type=jnp.float32
    )
    heads_out = attended.astype(jnp.bfloat16).reshape(
        step_count * sessions, local_heads * group_size * HEAD_DIM
    )
    partial_out = jnp.dot(heads_out, out_weight, preferred_element_type=jnp.float32).reshape(
        step_count, sessions, out_weight.shape[1]
    )
    summed = lax.psum(partial_out, "tp")
    return (installed, appended, summed.astype(jnp.bfloat16))


def solution(mesh):
    in_specs = (
        P(None, "rep", None),
        P(None, "rep", "tp"),
        P("rep", "tp"),
        P(),
        P("rep", None, "tp"),
        P("rep", None, "tp"),
        P("rep"),
        P("tp", None),
    )
    out_specs = (P(None, "tp"), P(None, "rep", "tp"), P(None, "rep", None))
    return jax.shard_map(shards, mesh=mesh, in_specs=in_specs, out_specs=out_specs, check_vma=False)
```

profile of v0, /device:TPU:0, one launch (start us, length us, event | category | flops | bytes accessed | tf_op | source)
XLA Modules:
  0.0 122.0 jit_solution(18131523121973448299)
XLA Ops:
  7.2 0.0 all-gather.2.cloned.1.call-start
  7.2 0.7 all-gather.2.cloned.1.call-update
  7.9 0.7 compare_and_fusion
  8.6 0.1 broadcast_bitcast_fusion
  8.7 0.9 reshape.241
  9.5 0.7 reshape.244
  10.3 0.7 compare_select_fusion
  10.9 0.7 add_convert_fusion
  11.7 0.8 iota_compare_fusion
  12.4 3.5 %fusion.43 = (f32[2,2,8]{2,0,1:T(2,128)S(1)}, f32[2,2,1,8,8192]{4,3,0,1,2:T(8,128)S(1)}) fusion(bf16[2,2,8,128]{3,2,1,0:T(8,128)(2,1)S(1)} %reshape.244, bf16[2,8192,128]{2,1,0:T(8,128)(2,1)} %param.12, pred[2,8192]{1,0:T(4,128)(4,1)S(1)} %iota_compare_fusion), kind=kOutput, calls=%fused_computation.60 | convolution fusion | flops 67895264 | bytes 5267584 | tf_op jit(solution)/shard_map/tsgqd,scgd->tsgqc/dot_general | solution.py:48
  15.9 33.7 %all-gather.2.cloned.1.call-done = bf16[8192,256]{1,0:T(8,128)(2,1)} async-done(((bf16[512,256]{1,0:T(8,128)(2,1)}), bf16[8192,256]{1,0:T(8,128)(2,1)}) %all-gather.2.cloned.1.call-update) | async-done | bytes 4194320 | tf_op jit(solution)/shard_map/all_gather | solution.py:35
  49.6 5.0 %gather_fusion = bf16[16,512,256]{2,1,0:T(8,128)(2,1)} fusion(bf16[16,512,256]{2,1,0:T(8,128)(2,1)} %bitcast.95, s32[1024]{0:T(1024)S(1)} %pad_clamp_fusion), kind=kCustom, calls=%fused_computation | custom fusion | bytes 8388672 | tf_op jit(solution)/shard_map/jit(_take)/gather | solution.py:36
  54.6 2.6 %broadcast_select_fusion = bf16[16,512,256]{2,1,0:T(8,128)(2,1)S(1)} fusion(bf16[16,512,256]{2,1,0:T(8,128)(2,1)} %gather_fusion, pred[16]{0:T(512)(128)(4,1)S(1)} %compare_and_fusion), kind=kLoop, calls=%fused_computation.11 | loop fusion | flops 2097152 | bytes 8388624 | tf_op jit(solution)/shard_map/jit(_take)/select_n | solution.py:36
  57.3 0.7 convolution_bitcast_fusion
  58.0 5.2 %bitcast_select_fusion = bf16[8192,256]{1,0:T(8,128)(2,1)} fusion(bf16[16,512,256]{2,1,0:T(8,128)(2,1)} %gather_fusion, pred[8192]{0:T(1024)(128)(4,1)S(1)} %bitcast.96), kind=kLoop, calls=%fused_computation.10 | loop fusion | flops 2097152 | bytes 8396800 | tf_op jit(solution)/shard_map/jit(_take)/select_n | solution.py:36
  63.2 0.1 fusion.36
  63.3 0.1 pad_maximum_fusion
  63.4 0.6 reshape.243
  64.0 0.2 convolution_multiply_fusion.1
  64.2 0.1 fusion.42
  64.3 0.1 fusion.26
  64.4 0.3 fusion.20
  64.7 0.1 fusion.37
  64.8 0.2 fusion.33
  65.0 2.9 %fusion.17 = bf16[2,2,1,8,128]{4,3,0,1,2:T(8,128)(2,1)S(1)} fusion(f32[2,128,2,8]{1,3,2,0:T(8,128)S(1)} %fusion.33, bf16[2,8192,128]{2,1,0:T(8,128)(2,1)} %param.13, f32[2,2,1,8,8192]{4,3,0,1,2:T(8,128)S(1)} %get-tuple-element.6, f32[2,2,8]{2,0,1:T(2,128)S(1)} %add.40, f32[2,2,8]{2,0,1:T(2,128)S(1)} %max.9), kind=kOutput, calls=%fused_computation.15 | convolution fusion | flops 67903488 | bytes 5267712 | tf_op jit(solution)/shard_map/tsgqc,scgd->tsgqd/dot_general | solution.py:78
  68.0 4.6 %fusion.3 = f32[2,2,4096]{2,1,0:T(2,128)S(1)} fusion(bf16[1024,4096]{1,0:T(8,128)(2,1)} %param.15, bf16[2,2,1024]{2,0,1:T(2,128)(2,1)S(1)} %dot_general.31), kind=kOutput, calls=%fused_computation.5 | convolution fusion | flops 33554432 | bytes 8462336 | tf_op jit(solution)/shard_map/dot_general | solution.py:87
  72.6 42.6 %psum.7 = bf16[2,2,4096]{2,1,0:T(2,128)(2,1)} all-reduce(f32[2,2,4096]{2,1,0:T(2,128)S(1)} %fusion.3), channel_id=1, replica_groups=mesh['rep'=16,'tp'=8] {'tp'}, use_global_device_ids=true, to_apply=%region_4.5 | all-reduce | flops 16384 | bytes 98304 | tf_op jit(solution)/shard_map/psum | solution.py:90
  (13 shorter events, 0.1 us)
Async XLA Ops:
  7.2 42.5 %all-gather.2.cloned.1.call-start = ((), (), s32[]{:S(2)}) async-start(), calls=%async_computation | async-start | bytes 4456448 | tf_op jit(solution)/shard_map/all_gather | solution.py:35
Sparse Core Ops, SparseCore 0:
  9.7 39.8 all-gather.1
where the time goes:
time: 123 us; the launch traced here: 122 us
  blocking collectives  42.6 us (35%)
  waiting for transfers between devices  34.4 us (28%)
  between operations  14.1 us (11%)
  matrix products  12 us (10%)
  other arithmetic  11.5 us (9%)
  local copies, waits for them, and re-layouts  7.29 us (6%)
    psum x1, blocking collectives, shards(): summed = lax.psum(partial_out, 'tp')  42.6 us
    all_gather x1, waiting for transfers between devices, shards(): pooled = lax.all_gather(sectioned, 'rep', axis=0, tiled=True)  33.7 us
    select_n x3, other arithmetic, shards(): jnp.take(pooled.reshape(replicas, block_rows, columns), owners, axis=0)  8.55 us
    gather x1, local copies, waits for them, and re-layouts, shards(): jnp.take(pooled.reshape(replicas, block_rows, columns), owners, axis=0)  4.97 us
    dot_general x1, matrix products, shards(): jnp.dot(heads_out, out_weight, preferred_element_type=jnp.float32)  4.64 us
    dot_general x1, matrix products, shards(): jnp.einsum('tsgqd,scgd->tsgqc', query_head_rows, stored_keys, preferred_e...  3.48 us
    dot_general x1, matrix products, shards(): jnp.einsum('tsgqc,scgd->tsgqd', weights_cache, stored_values, preferred_e...  2.92 us
  transfers between devices with their start and end apart: 1, of which 1 were waited for; matrix products, arithmetic and copies ran while one was open for 7% of the time, Pallas kernels for 0%

commit v1 on v0

v1 whole, which is shorter than its diff:
```python
import functools
import math

import jax
import jax.numpy as jnp
from jax import lax
from jax.experimental import pallas as pl
from jax.experimental.pallas import tpu as pltpu
from jax.sharding import PartitionSpec as P

HEAD_DIM = 128
ROPE_BASE = 500000.0
SCALE = HEAD_DIM**-0.5
MESH = pl.DeviceIdType.MESH
F32 = jnp.float32
BF16 = jnp.bfloat16

REPS = 16
TPS = 8
ROWS = 512
COLS = 256
STEPS = 2
SESSIONS = 2
TOKENS = STEPS * SESSIONS
GROUP = 8
QROWS = STEPS * GROUP
SLOTS = 8192
CHUNK = 2048
OUT_COLS = 512

A0 = (0, 144)
A1 = (144, 144)
A = (0, 288)
B0 = (288, 112)
B1 = (400, 112)
B = (288, 224)
WHOLE = (0, 512)


def frequencies(shape):
    lane = lax.broadcasted_iota(jnp.int32, shape, 1) % (HEAD_DIM // 2)
    result = jnp.ones(shape, F32)
    for bit in range(6):
        factor = math.exp(-math.log(ROPE_BASE) * (1 << bit) / (HEAD_DIM // 2))
        result = result * jnp.where((lane // (1 << bit)) % 2 == 1, factor, 1.0).astype(F32)
    return result


def main_kernel(
    hidden, queries, sectioned, owners, keys, values, lengths, weight,
    pooled, attended, appended,
    kbuf, vbuf, wbuf, hbuf, qbuf, own_s, len_s, hsplit, hsend, hrecv, hall, psend, precv,
    qrows, scores, heads, lhs, rsend, rrecv, gsend,
    load_sem, bulk_send, bulk_recv, sib_recv, small_send, small_recv,
):
    rep = lax.axis_index("rep")
    tp = lax.axis_index("tp")
    y, z, c = rep // 8, (rep // 2) % 4, rep % 2

    def chip(yy, zz, cc):
        return yy * 8 + lax.rem(zz + 4, 4) * 2 + cc

    zp = (chip(y, z + 1, c), tp)
    zm = (chip(y, z - 1, c), tp)
    yn = (chip(1 - y, z, c), tp)
    sib = (chip(y, z, 1 - c), tp)

    barrier = pltpu.get_barrier_semaphore()
    for k in range(1, REPS):
        pl.semaphore_signal(barrier, inc=1, device_id=(lax.rem(rep + k, REPS), tp), device_id_type=MESH)
    for k in range(1, TPS):
        pl.semaphore_signal(barrier, inc=1, device_id=(rep, lax.rem(tp + k, TPS)), device_id_type=MESH)

    loads = [
        pltpu.make_async_copy(owners, own_s, load_sem.at[0]),
        pltpu.make_async_copy(hidden, hbuf, load_sem.at[1]),
        pltpu.make_async_copy(sectioned, pooled.at[rep], load_sem.at[2]),
        pltpu.make_async_copy(lengths, len_s, load_sem.at[3]),
        pltpu.make_async_copy(queries, qbuf, load_sem.at[4]),
        pltpu.make_async_copy(keys.at[0], kbuf.at[0], load_sem.at[5]),
        pltpu.make_async_copy(keys.at[1], kbuf.at[1], load_sem.at[6]),
        pltpu.make_async_copy(values.at[0], vbuf.at[0], load_sem.at[7]),
        pltpu.make_async_copy(values.at[1], vbuf.at[1], load_sem.at[8]),
        pltpu.make_async_copy(weight, wbuf, load_sem.at[9]),
    ]
    for load in loads:
        load.start()

    loads[0].wait()
    loads[1].wait()
    for s in range(REPS):
        for t in range(STEPS):
            hsplit[s, pl.ds(t * SESSIONS, SESSIONS), :] = hbuf[t, :, pl.ds(s * ROWS, ROWS)].astype(F32)
    owner = [own_s[s] for s in range(REPS)]
    for r in range(REPS):
        place = jnp.int32(0)
        for s in range(1, REPS):
            place = jnp.where(owner[s] == r, s, place)
        hsend[r] = hsplit[place].astype(BF16)

    loads[4].wait()
    for s in range(SESSIONS):
        for t in range(STEPS):
            for q in range(GROUP):
                qrows[s, pl.ds(t * GROUP + q, 1), :] = qbuf[t, pl.ds(s, 1), pl.ds(q * HEAD_DIM, HEAD_DIM)].astype(F32)
    loads[2].wait()
    pl.semaphore_wait(barrier, REPS - 1 + TPS - 1)

    def small(src, dst, which, device):
        return pltpu.make_async_remote_copy(
            src_ref=src, dst_ref=dst, send_sem=small_send.at[which], recv_sem=small_recv.at[which],
            device_id=device, device_id_type=MESH)

    for k in range(1, REPS):
        peer = lax.rem(rep + k, REPS)
        small(hsend.at[peer], hrecv.at[rep], 0, (peer, tp)).start()
    hrecv[rep] = hsend[rep]

    def piece(block, part):
        return pooled.at[block, pl.ds(*part), :]

    def send(block, part, device, slot):
        ref = piece(block, part)
        pltpu.make_async_remote_copy(
            src_ref=ref, dst_ref=ref, send_sem=bulk_send, recv_sem=bulk_recv.at[slot],
            device_id=device, device_id_type=MESH).start()

    def to_sibling(block, part):
        ref = piece(block, part)
        pltpu.make_async_remote_copy(
            src_ref=ref, dst_ref=ref, send_sem=bulk_send, recv_sem=sib_recv,
            device_id=sib, device_id_type=MESH).start()

    def arrived(block, part, slot):
        ref = piece(block, part)
        pltpu.make_async_copy(ref, ref, bulk_recv.at[slot]).wait()

    here = {
        0: chip(y, z, c), 1: chip(y, z + 1, c), -1: chip(y, z - 1, c), 2: chip(y, z + 2, c)}
    there = {
        0: chip(1 - y, z, c), 1: chip(1 - y, z + 1, c), -1: chip(1 - y, z - 1, c), 2: chip(1 - y, z + 2, c)}

    send(here[0], B, zp, 1)
    send(here[0], B, zm, 2)
    send(here[0], A, yn, 3)
    send(here[0], A, zp, 4)
    send(here[0], A, zm, 5)
    send(here[0], B, yn, 14)
    to_sibling(here[0], WHOLE)

    def event(n):
        if n == 1:
            arrived(here[-1], B, 1)
            send(here[-1], B0, zp, 6)
            send(here[-1], B, yn, 15)
            to_sibling(here[-1], B)
        elif n == 2:
            arrived(here[1], B, 2)
            send(here[1], B1, zm, 7)
            send(here[1], B, yn, 16)
            to_sibling(here[1], B)
        elif n == 3:
            arrived(there[0], A, 3)
            send(there[0], A, zp, 8)
            send(there[0], A, zm, 9)
            to_sibling(there[0], A)
        elif n == 4:
            arrived(here[-1], A, 4)
            send(here[-1], A0, zp, 10)
            to_sibling(here[-1], A)
        elif n == 5:
            arrived(here[1], A, 5)
            send(here[1], A1, zm, 11)
            to_sibling(here[1], A)
        elif n == 6:
            arrived(here[2], B0, 6)
            send(here[2], B0, yn, 17)
            to_sibling(here[2], B0)
        elif n == 7:
            arrived(here[2], B1, 7)
            send(here[2], B1, yn, 18)
            to_sibling(here[2], B1)
        elif n == 8:
            arrived(there[-1], A, 8)
            send(there[-1], A0, zp, 12)
            to_sibling(there[-1], A)
        elif n == 9:
            arrived(there[1], A, 9)
            send(there[1], A1, zm, 13)
            to_sibling(there[1], A)
        else:
            block, part = {
                10: (here[2], A0), 11: (here[2], A1), 12: (there[2], A0), 13: (there[2], A1), 14: (there[0], B),
                15: (there[-1], B), 16: (there[1], B), 17: (there[2], B0), 18: (there[2], B1)}[n]
            arrived(block, part, n)
            to_sibling(block, part)

    loads[3].wait()
    length = [len_s[s] for s in range(SESSIONS)]

    def score(s):
        loads[5 + s].wait()
        q = qrows[s].astype(BF16)
        largest = jnp.full((QROWS, HEAD_DIM), -jnp.inf, F32)
        for i in range(SLOTS // CHUNK):
            part = lax.dot_general(
                q, kbuf[s, pl.ds(i * CHUNK, CHUNK), :], (((1,), (1,)), ((), ())), preferred_element_type=F32) * SCALE
            slot = lax.broadcasted_iota(jnp.int32, (QROWS, CHUNK), 1) + i * CHUNK
            part = jnp.where(slot < length[s], part, -jnp.inf)
            scores[s, :, pl.ds(i * CHUNK, CHUNK)] = part
            for j in range(CHUNK // HEAD_DIM):
                largest = jnp.maximum(largest, part[:, j * HEAD_DIM : (j + 1) * HEAD_DIM])
        return jnp.max(largest, axis=1, keepdims=True)

    def weigh(s, top):
        loads[7 + s].wait()
        total = jnp.zeros((QROWS, HEAD_DIM), F32)
        acc = jnp.zeros((QROWS, HEAD_DIM), F32)
        for i in range(SLOTS // CHUNK):
            p = jnp.exp(scores[s, :, pl.ds(i * CHUNK, CHUNK)] - top)
            for j in range(CHUNK // HEAD_DIM):
                total = total + p[:, j * HEAD_DIM : (j + 1) * HEAD_DIM]
            acc = acc + jnp.dot(p.astype(BF16), vbuf[s, pl.ds(i * CHUNK, CHUNK), :], preferred_element_type=F32)
        return jnp.sum(total, axis=1, keepdims=True), acc

    top = [None, None]
    total = [None, None]
    acc = [None, None]
    top[0] = score(0)
    top[1] = score(1)

    pltpu.make_async_copy(hrecv.at[pl.ds(0, REPS - 1)], hrecv.at[pl.ds(0, REPS - 1)], small_recv.at[0]).wait()
    for r in range(REPS):
        hall[pl.ds(r * TOKENS, TOKENS), :] = hrecv[r].astype(F32)
    product = jnp.dot(hall[...].astype(BF16), pooled[rep], preferred_element_type=F32)
    for r in range(REPS):
        psend[r] = product[r * TOKENS : (r + 1) * TOKENS, :]
    for k in range(1, REPS):
        peer = lax.rem(rep + k, REPS)
        small(psend.at[peer], precv.at[rep], 1, (peer, tp)).start()
    precv[rep] = psend[rep]

    total[0], acc[0] = weigh(0, top[0])
    event(1)
    event(2)
    event(3)
    total[1], acc[1] = weigh(1, top[1])
    event(4)
    event(5)

    pltpu.make_async_copy(precv.at[pl.ds(0, REPS - 1)], precv.at[pl.ds(0, REPS - 1)], small_recv.at[1]).wait()
    projected = precv[0]
    for r in range(1, REPS):
        projected = projected + precv[r]
    row = lax.broadcasted_iota(jnp.int32, (TOKENS, HEAD_DIM), 0)
    lane = lax.broadcasted_iota(jnp.int32, (TOKENS, HEAD_DIM), 1)
    position = jnp.where(row % 2 == 0, length[0], length[1]) + row // 2
    angle = position.astype(F32) * frequencies((TOKENS, HEAD_DIM))
    raw = projected[:, :HEAD_DIM]
    swapped = jnp.concatenate([raw[:, HEAD_DIM // 2 :], raw[:, : HEAD_DIM // 2]], axis=1)
    sine = jnp.where(lane < HEAD_DIM // 2, -jnp.sin(angle), jnp.sin(angle))
    new_keys = (raw * jnp.cos(angle) + swapped * sine).astype(BF16)
    new_values = projected[:, HEAD_DIM:].astype(BF16)
    for t in range(STEPS):
        appended[t, :, pl.ds(0, HEAD_DIM)] = new_keys[t * SESSIONS : (t + 1) * SESSIONS, :]
        appended[t, :, pl.ds(HEAD_DIM, HEAD_DIM)] = new_values[t * SESSIONS : (t + 1) * SESSIONS, :]
    new_keys = new_keys.astype(F32)
    new_values = new_values.astype(F32)
    second = lax.broadcasted_iota(jnp.int32, (QROWS, 1), 0) >= GROUP
    for s in range(SESSIONS):
        q = qrows[s]
        fresh = [
            jnp.sum(q * new_keys[u * SESSIONS + s : u * SESSIONS + s + 1, :], axis=1, keepdims=True) * SCALE
            for u in range(STEPS)]
        fresh[1] = jnp.where(second, fresh[1], -jnp.inf)
        peak = jnp.maximum(top[s], jnp.maximum(fresh[0], fresh[1]))
        keep = jnp.exp(top[s] - peak)
        fresh = [jnp.exp(x - peak) for x in fresh]
        whole = total[s] * keep + fresh[0] + fresh[1]
        out = acc[s] * (keep / whole)
        for u in range(STEPS):
            out = out + (fresh[u] / whole).astype(BF16).astype(F32) * new_values[u * SESSIONS + s : u * SESSIONS + s + 1, :]
        heads[s] = out
    lhs[...] = jnp.zeros(lhs.shape, F32)
    for s in range(SESSIONS):
        for t in range(STEPS):
            for q in range(GROUP):
                lhs[pl.ds(t * SESSIONS + s, 1), pl.ds(q * HEAD_DIM, HEAD_DIM)] = heads[s, pl.ds(t * GROUP + q, 1), :]
    left = lhs[...].astype(BF16)
    loads[9].wait()
    for k in range(1, TPS + 1):
        peer = lax.rem(tp + k, TPS)
        columns = pl.ds(pl.multiple_of(peer * OUT_COLS, OUT_COLS), OUT_COLS)
        part = jnp.dot(left, wbuf[:, columns], preferred_element_type=F32)[:TOKENS]
        if k == TPS:
            rrecv[tp] = part
        else:
            rsend[k] = part
            small(rsend.at[k], rrecv.at[tp], 2, (rep, peer)).start()
    event(6)
    event(7)
    event(8)
    event(9)
    event(14)

    pltpu.make_async_copy(rrecv.at[pl.ds(0, TPS - 1)], rrecv.at[pl.ds(0, TPS - 1)], small_recv.at[2]).wait()
    summed = rrecv[0]
    for r in range(1, TPS):
        summed = summed + rrecv[r]
    summed = summed.astype(BF16)
    mine = pl.ds(pl.multiple_of(tp * OUT_COLS, OUT_COLS), OUT_COLS)
    for t in range(STEPS):
        gsend[t] = summed[t * SESSIONS : (t + 1) * SESSIONS, :]
        attended[t, :, mine] = summed[t * SESSIONS : (t + 1) * SESSIONS, :]
    for k in range(1, TPS):
        small(gsend, attended.at[:, :, mine], 3, (rep, lax.rem(tp + k, TPS))).start()

    for n in (15, 16, 10, 11, 17, 18, 12, 13):
        event(n)

    def drain(ref, sem):
        pltpu.make_async_copy(ref, ref, sem).wait()

    others = attended.at[:, :, pl.ds(0, (TPS - 1) * OUT_COLS)]
    drain(others, small_recv.at[3])
    drain(pooled.at[pl.ds(0, REPS // 2)], sib_recv)
    drain(pooled.at[pl.ds(0, REPS - 1)], bulk_send)
    drain(hsend.at[pl.ds(0, REPS - 1)], small_send.at[0])
    drain(psend.at[pl.ds(0, REPS - 1)], small_send.at[1])
    drain(rsend.at[pl.ds(0, TPS - 1)], small_send.at[2])
    drain(others, small_send.at[3])


def write_kernel(owners, pooled, attended, appended, installed, attended_out, appended_out, sem):
    copies = [
        pltpu.make_async_copy(pooled.at[owners[s]], installed.at[s], sem.at[s]) for s in range(REPS)]
    copies.append(pltpu.make_async_copy(attended, attended_out, sem.at[REPS]))
    copies.append(pltpu.make_async_copy(appended, appended_out, sem.at[REPS + 1]))
    for copy in copies:
        copy.start()
    for copy in copies:
        copy.wait()


def shards(hidden, queries, sectioned, owners, keys, values, lengths, weight):
    hbm = pl.BlockSpec(memory_space=pltpu.HBM)
    vmem = pl.BlockSpec(memory_space=pltpu.VMEM)
    pooled, attended, appended = pl.pallas_call(
        main_kernel,
        out_shape=(
            pltpu.VMEM((REPS, ROWS, COLS), BF16),
            pltpu.VMEM((STEPS, SESSIONS, TPS * OUT_COLS), BF16),
            pltpu.VMEM((STEPS, SESSIONS, COLS), BF16),
        ),
        in_specs=[hbm] * 8,
        out_specs=(vmem, vmem, vmem),
        scratch_shapes=[
            pltpu.VMEM((SESSIONS, SLOTS, HEAD_DIM), BF16),
            pltpu.VMEM((SESSIONS, SLOTS, HEAD_DIM), BF16),
            pltpu.VMEM((GROUP * HEAD_DIM, TPS * OUT_COLS), BF16),
            pltpu.VMEM((STEPS, SESSIONS, REPS * ROWS), BF16),
            pltpu.VMEM((STEPS, SESSIONS, GROUP * HEAD_DIM), BF16),
            pltpu.SMEM((REPS,), jnp.int32),
            pltpu.SMEM((SESSIONS,), jnp.int32),
            pltpu.VMEM((REPS, TOKENS, ROWS), F32),
            pltpu.VMEM((REPS, TOKENS, ROWS), BF16),
            pltpu.VMEM((REPS, TOKENS, ROWS), BF16),
            pltpu.VMEM((REPS * TOKENS, ROWS), F32),
            pltpu.VMEM((REPS, TOKENS, COLS), F32),
            pltpu.VMEM((REPS, TOKENS, COLS), F32),
            pltpu.VMEM((SESSIONS, QROWS, HEAD_DIM), F32),
            pltpu.VMEM((SESSIONS, QROWS, SLOTS), F32),
            pltpu.VMEM((SESSIONS, QROWS, HEAD_DIM), F32),
            pltpu.VMEM((8, GROUP * HEAD_DIM), F32),
            pltpu.VMEM((TPS, TOKENS, OUT_COLS), F32),
            pltpu.VMEM((TPS, TOKENS, OUT_COLS), F32),
            pltpu.VMEM((STEPS, SESSIONS, OUT_COLS), BF16),
            pltpu.SemaphoreType.DMA((10,)),
            pltpu.SemaphoreType.DMA,
            pltpu.SemaphoreType.DMA((19,)),
            pltpu.SemaphoreType.DMA,
            pltpu.SemaphoreType.DMA((4,)),
            pltpu.SemaphoreType.DMA((4,)),
        ],
        compiler_params=pltpu.CompilerParams(
            collective_id=0, has_side_effects=True, vmem_limit_bytes=32 << 20),
        name="gather_and_attend",
    )(hidden, queries, sectioned, owners, keys, values, lengths, weight)
    installed, attended, appended = pl.pallas_call(
        write_kernel,
        out_shape=(
            jax.ShapeDtypeStruct((REPS, ROWS, COLS), BF16),
            jax.ShapeDtypeStruct(attended.shape, BF16),
            jax.ShapeDtypeStruct(appended.shape, BF16),
        ),
        grid_spec=pltpu.PrefetchScalarGridSpec(
            num_scalar_prefetch=1,
            grid=(),
            in_specs=[vmem, vmem, vmem],
            out_specs=(hbm, hbm, hbm),
            scratch_shapes=[pltpu.SemaphoreType.DMA((REPS + 2,))],
        ),
        compiler_params=pltpu.CompilerParams(vmem_limit_bytes=4 << 20),
        name="write_in_order",
    )(owners, pooled, attended, appended)
    return installed.reshape(REPS * ROWS, COLS), appended, attended


def solution(mesh):
    in_specs = (
        P(None, "rep", None),
        P(None, "rep", "tp"),
        P("rep", "tp"),
        P(),
        P("rep", None, "tp"),
        P("rep", None, "tp"),
        P("rep"),
        P("tp", None),
    )
    out_specs = (P(None, "tp"), P(None, "rep", "tp"), P(None, "rep", None))
    return jax.shard_map(shards, mesh=mesh, in_specs=in_specs, out_specs=out_specs, check_vma=False)
```

time: 123 us -> 44.6 us (0.36)
  blocking collectives: 42.6 us -> 0 us
  waiting for transfers between devices: 34.4 us -> 0 us
  Pallas kernels: 0 us -> 32.1 us
  between operations: 14.1 us -> 0.66 us
  matrix products: 12 us -> 0 us
  other arithmetic: 11.5 us -> 0 us
  local copies, waits for them, and re-layouts: 7.29 us -> 11.5 us
    psum x1 -> x0, blocking collectives: 42.6 us -> none  [shards(): summed = lax.psum(partial_out, 'tp')]
    all_gather x1 -> x0, waiting for transfers between devices: 33.7 us -> none  [shards(): pooled = lax.all_gather(sectioned, 'rep', axis=0, tiled=True)]
    pallas_call x0 -> x2, Pallas kernels: none -> 32.1 us  [the longest x1 29.4 us: shards(): pl.pallas_call(main_kernel, out_shape=(pltpu.VMEM((REPS, ROWS, COLS), BF1...]
    dot_general x6 -> x0, matrix products: 12 us -> none  [the longest x1 4.64 us: shards(): jnp.dot(heads_out, out_weight, preferred_element_type=jnp.float32)]
    unnamed x4 -> x16, local copies, waits for them, and re-layouts: 0.1 us -> 11.5 us
    select_n x3 -> x0, other arithmetic: 8.55 us -> none  [shards(): jnp.take(pooled.reshape(replicas, block_rows, columns), owners, axis=0)]
    gather x1 -> x0, local copies, waits for them, and re-layouts: 4.97 us -> none  [shards(): jnp.take(pooled.reshape(replicas, block_rows, columns), owners, axis=0)]
    reshape x3 -> x0, local copies, waits for them, and re-layouts: 1.48 us -> none  [the longest x1 0.87 us: shards(): flat_hidden = hidden.reshape(step_count * sessions, model_width)]
  transfers between devices with their start and end apart: 1 -> 0, of which waited for: 1 -> 0; matrix products, arithmetic and copies ran while one was open for 7% -> 0% of each run, Pallas kernels for 0% -> 0%
where the time goes in v1:
time: 44.6 us; the launch traced here: 44.3 us
  Pallas kernels  32.1 us (72%)
  local copies, waits for them, and re-layouts  11.5 us (26%)
  between operations  0.66 us (1%)
    pallas_call x1, Pallas kernels, shards(): pl.pallas_call(main_kernel, out_shape=(pltpu.VMEM((REPS, ROWS, COLS), BF1...  29.4 us
    unnamed x16, local copies, waits for them, and re-layouts  11.5 us
    pallas_call x1, Pallas kernels, shards(): pl.pallas_call(write_kernel, out_shape=(jax.ShapeDtypeStruct((REPS, ROWS,...  2.7 us

profile of v1, /device:TPU:0, one launch (start us, length us, event | category | flops | bytes accessed | tf_op | source)
XLA Modules:
  0.0 44.3 jit_solution(546880995677018618)
XLA Ops:
  0.6 0.0 copy-start
  0.6 3.4 %copy-done = bf16[1024,4096]{1,0:T(8,128)(2,1)S(1)} copy-done((bf16[1024,4096]{1,0:T(8,128)(2,1)S(1)}, bf16[1024,4096]{1,0:T(8,128)(2,1)}, u32[]{:S(2)}) %copy-start) | copy-done | bytes 8388632
  4.0 0.0 copy-start.1
  4.0 2.2 %copy-done.1 = bf16[2,8192,128]{2,1,0:T(8,128)(2,1)S(1)} copy-done((bf16[2,8192,128]{2,1,0:T(8,128)(2,1)S(1)}, bf16[2,8192,128]{2,1,0:T(8,128)(2,1)}, u32[]{:S(2)}) %copy-start.1) | copy-done | bytes 4194328
  6.2 0.0 copy-start.2
  6.2 2.2 %copy-done.2 = bf16[2,8192,128]{2,1,0:T(8,128)(2,1)S(1)} copy-done((bf16[2,8192,128]{2,1,0:T(8,128)(2,1)S(1)}, bf16[2,8192,128]{2,1,0:T(8,128)(2,1)}, u32[]{:S(2)}) %copy-start.2) | copy-done | bytes 4194328
  8.4 0.0 copy-start.3
  8.4 0.9 %copy-done.3 = bf16[512,256]{1,0:T(8,128)(2,1)S(1)} copy-done((bf16[512,256]{1,0:T(8,128)(2,1)S(1)}, bf16[512,256]{1,0:T(8,128)(2,1)}, u32[]{:S(2)}) %copy-start.3) | copy-done | bytes 262168
  9.3 0.0 copy-start.4
  9.3 0.8 %copy-done.4 = bf16[2,2,8192]{2,1,0:T(2,128)(2,1)S(1)} copy-done((bf16[2,2,8192]{2,1,0:T(2,128)(2,1)S(1)}, bf16[2,2,8192]{2,1,0:T(2,128)(2,1)}, u32[]{:S(2)}) %copy-start.4) | copy-done | bytes 65560
  10.2 0.0 copy-start.5
  10.2 0.7 %copy-done.5 = bf16[2,2,1024]{2,1,0:T(2,128)(2,1)S(1)} copy-done((bf16[2,2,1024]{2,1,0:T(2,128)(2,1)S(1)}, bf16[2,2,1024]{2,1,0:T(2,128)(2,1)}, u32[]{:S(2)}) %copy-start.5) | copy-done | bytes 8216
  10.9 0.0 copy-start.6
  10.9 0.7 %copy-done.6 = s32[16]{0:T(128)S(1)} copy-done((s32[16]{0:T(128)S(1)}, s32[16]{0:T(128)}, u32[]{:S(2)}) %copy-start.6) | copy-done | bytes 88
  11.5 0.0 copy-start.7
  11.5 0.7 %copy-done.7 = s32[2]{0:T(128)S(1)} copy-done((s32[2]{0:T(128)S(1)}, s32[2]{0:T(128)}, u32[]{:S(2)}) %copy-start.7) | copy-done | bytes 32
  12.2 29.4 %gather_and_attend.1 = (bf16[16,512,256]{2,1,0:T(8,128)(2,1)S(1)}, bf16[2,2,4096]{2,1,0:T(2,128)(2,1)S(1)}, bf16[2,2,256]{2,1,0:T(2,128)(2,1)S(1)}) custom-call(bf16[2,2,8192]{2,1,0:T(2,128)(2,1)S(1)} %copy-done.4, bf16[2,2,1024]{2,1,0:T(2,128)(2,1)S(1)} %copy-done.5, bf16[512,256]{1,0:T(8,128)(2,1)S(1)} %copy-done.3, s32[16]{0:T(128)S(1)} %copy-done.6, ...), custom_call_target="tpu_custom_call" | custom-call | tf_op jit(solution)/shard_map/gather_and_attend/pallas_call | solution.py:348
  41.6 2.7 %write_in_order.1 = (bf16[16,512,256]{2,1,0:T(8,128)(2,1)}, bf16[2,2,4096]{2,1,0:T(2,128)(2,1)}, bf16[2,2,256]{2,1,0:T(2,128)(2,1)}) custom-call(s32[16]{0:T(128)S(1)} %copy-done.6, bf16[16,512,256]{2,1,0:T(8,128)(2,1)S(1)} %get-tuple-element.9.pooled, bf16[2,2,4096]{2,1,0:T(2,128)(2,1)S(1)} %get-tuple-element.10.attended, ...), custom_call_target="tpu_custom_call" | custom-call | tf_op jit(solution)/shard_map/write_in_order/pallas_call | solution.py:389
Async XLA Ops:
  0.6 3.4 %copy-start = (bf16[1024,4096]{1,0:T(8,128)(2,1)S(1)}, bf16[1024,4096]{1,0:T(8,128)(2,1)}, u32[]{:S(2)}) copy-start(bf16[1024,4096]{1,0:T(8,128)(2,1)} %weight.1) | copy-start | bytes 25165828
  4.0 2.2 %copy-start.1 = (bf16[2,8192,128]{2,1,0:T(8,128)(2,1)S(1)}, bf16[2,8192,128]{2,1,0:T(8,128)(2,1)}, u32[]{:S(2)}) copy-start(bf16[2,8192,128]{2,1,0:T(8,128)(2,1)} %keys.1) | copy-start | bytes 12582916
  6.2 2.2 %copy-start.2 = (bf16[2,8192,128]{2,1,0:T(8,128)(2,1)S(1)}, bf16[2,8192,128]{2,1,0:T(8,128)(2,1)}, u32[]{:S(2)}) copy-start(bf16[2,8192,128]{2,1,0:T(8,128)(2,1)} %values.1) | copy-start | bytes 12582916
  8.4 0.9 %copy-start.3 = (bf16[512,256]{1,0:T(8,128)(2,1)S(1)}, bf16[512,256]{1,0:T(8,128)(2,1)}, u32[]{:S(2)}) copy-start(bf16[512,256]{1,0:T(8,128)(2,1)} %sectioned.1) | copy-start | bytes 786436
  9.3 0.8 %copy-start.4 = (bf16[2,2,8192]{2,1,0:T(2,128)(2,1)S(1)}, bf16[2,2,8192]{2,1,0:T(2,128)(2,1)}, u32[]{:S(2)}) copy-start(bf16[2,2,8192]{2,1,0:T(2,128)(2,1)} %hidden.1) | copy-start | bytes 196612
  10.2 0.7 %copy-start.5 = (bf16[2,2,1024]{2,1,0:T(2,128)(2,1)S(1)}, bf16[2,2,1024]{2,1,0:T(2,128)(2,1)}, u32[]{:S(2)}) copy-start(bf16[2,2,1024]{2,1,0:T(2,128)(2,1)} %queries.1) | copy-start | bytes 24580
  10.9 0.7 %copy-start.6 = (s32[16]{0:T(128)S(1)}, s32[16]{0:T(128)}, u32[]{:S(2)}) copy-start(s32[16]{0:T(128)} %owners.3) | copy-start | bytes 196
  11.5 0.7 %copy-start.7 = (s32[2]{0:T(128)S(1)}, s32[2]{0:T(128)}, u32[]{:S(2)}) copy-start(s32[2]{0:T(128)} %lengths.1) | copy-start | bytes 28

commit v2 on v1

v2 whole, which is shorter than its diff:
```python
import functools
import math

import jax
import jax.numpy as jnp
from jax import lax
from jax.experimental import pallas as pl
from jax.experimental.pallas import tpu as pltpu
from jax.sharding import PartitionSpec as P

HEAD_DIM = 128
ROPE_BASE = 500000.0
SCALE = HEAD_DIM**-0.5
MESH = pl.DeviceIdType.MESH
F32 = jnp.float32
BF16 = jnp.bfloat16

REPS = 16
TPS = 8
ROWS = 512
COLS = 256
STEPS = 2
SESSIONS = 2
TOKENS = STEPS * SESSIONS
GROUP = 8
QROWS = STEPS * GROUP
SLOTS = 8192
CHUNK = 2048
OUT_COLS = 512
HALF = 2048

A0 = (0, 160)
A1 = (160, 176)
A = (0, 336)
B0 = (336, 80)
B1 = (416, 96)
B = (336, 176)
WHOLE = (0, 512)


def frequencies(shape):
    lane = lax.broadcasted_iota(jnp.int32, shape, 1) % (HEAD_DIM // 2)
    result = jnp.ones(shape, F32)
    for bit in range(6):
        factor = math.exp(-math.log(ROPE_BASE) * (1 << bit) / (HEAD_DIM // 2))
        result = result * jnp.where((lane // (1 << bit)) % 2 == 1, factor, 1.0).astype(F32)
    return result


def main_kernel(
    hidden, queries, sectioned, owners, keys, values, lengths, weight,
    pooled, attended, appended,
    kbuf, vbuf, wbuf, hbuf, qbuf, own_s, len_s, hsplit, hsend, hrecv, hall, psend, precv,
    qrows, scores, heads, lhs, osend, orecv,
    load_sem, bulk_send, bulk_recv, sib_recv, small_send, small_recv, ready,
):
    rep = lax.axis_index("rep")
    tp = lax.axis_index("tp")
    y, z, c = rep // 8, (rep // 2) % 4, rep % 2

    def chip(yy, zz, cc):
        return yy * 8 + lax.rem(zz + 4, 4) * 2 + cc

    zp = (chip(y, z + 1, c), tp)
    zm = (chip(y, z - 1, c), tp)
    yn = (chip(1 - y, z, c), tp)
    sib = (chip(y, z, 1 - c), tp)

    loads = [
        pltpu.make_async_copy(owners, own_s, load_sem.at[0]),
        pltpu.make_async_copy(hidden, hbuf, load_sem.at[1]),
        pltpu.make_async_copy(sectioned, pooled.at[rep], load_sem.at[2]),
        pltpu.make_async_copy(lengths, len_s, load_sem.at[3]),
        pltpu.make_async_copy(queries, qbuf, load_sem.at[4]),
        pltpu.make_async_copy(keys.at[0], kbuf.at[0], load_sem.at[5]),
        pltpu.make_async_copy(keys.at[1], kbuf.at[1], load_sem.at[6]),
        pltpu.make_async_copy(values.at[0], vbuf.at[0], load_sem.at[7]),
        pltpu.make_async_copy(values.at[1], vbuf.at[1], load_sem.at[8]),
        pltpu.make_async_copy(weight, wbuf, load_sem.at[9]),
    ]
    for load in loads[:5]:
        load.start()

    barrier = pltpu.get_barrier_semaphore()

    @pl.loop(0, REPS)
    def _(k):
        @pl.when((k != rep) & (k != 1))
        def _():
            pl.semaphore_signal(barrier, inc=1, device_id=(k, tp), device_id_type=MESH)

    loads[0].wait()

    loads[1].wait()
    for r in range(REPS):
        for t in range(STEPS):
            hsplit[r, t] = hbuf[t, :, pl.ds(r * ROWS, ROWS)]

    @pl.loop(0, REPS)
    def _(r):
        found = jnp.int32(0)
        for s in range(1, REPS):
            found = jnp.where(own_s[s] == r, s, found)
        hsend[r] = hsplit[found]

    loads[2].wait()
    for load in loads[5:]:
        load.start()

    @pl.when(rep != 1)
    def _():
        pl.semaphore_wait(barrier, REPS - 1)

    @pl.when(rep == 0)
    def _():
        pl.semaphore_signal(ready, inc=1, device_id=(1, tp), device_id_type=MESH)

        @pl.loop(1, TPS)
        def _(k):
            pl.semaphore_signal(barrier, inc=1, device_id=(1, lax.rem(tp + k, TPS)), device_id_type=MESH)

    @pl.when(rep == 1)
    def _():
        pl.semaphore_wait(ready, 1)

    def small(src, dst, which, device):
        return pltpu.make_async_remote_copy(
            src_ref=src, dst_ref=dst, send_sem=small_send.at[which], recv_sem=small_recv.at[which],
            device_id=device, device_id_type=MESH)

    @pl.loop(1, REPS)
    def _(k):
        peer = lax.rem(rep + k, REPS)
        small(hsend.at[peer], hrecv.at[rep], 0, (peer, tp)).start()

    hrecv[rep] = hsend[rep]

    def piece(block, part):
        return pooled.at[block, pl.ds(*part), :]

    def send(block, part, device, slot):
        ref = piece(block, part)
        pltpu.make_async_remote_copy(
            src_ref=ref, dst_ref=ref, send_sem=bulk_send, recv_sem=bulk_recv.at[slot],
            device_id=device, device_id_type=MESH).start()

    def to_sibling(block, part):
        ref = piece(block, part)
        pltpu.make_async_remote_copy(
            src_ref=ref, dst_ref=ref, send_sem=bulk_send, recv_sem=sib_recv,
            device_id=sib, device_id_type=MESH).start()

    def arrived(block, part, slot):
        ref = piece(block, part)
        pltpu.make_async_copy(ref, ref, bulk_recv.at[slot]).wait()

    here = {
        0: chip(y, z, c), 1: chip(y, z + 1, c), -1: chip(y, z - 1, c), 2: chip(y, z + 2, c)}
    there = {
        0: chip(1 - y, z, c), 1: chip(1 - y, z + 1, c), -1: chip(1 - y, z - 1, c), 2: chip(1 - y, z + 2, c)}

    def along(base, block, first, second):
        send(block, first, zp, base)
        send(block, second, zm, base + 2)

    def along_rest(base, block, first, second):
        send(block, second, zp, base + 1)
        send(block, first, zm, base + 3)

    def first_piece(base, row, first, second, down):
        block, part = (row[-1], first) if down else (row[1], second)
        arrived(block, part, base if down else base + 2)
        send(block, part, zp if down else zm, base + (4 if down else 5))
        return block, part

    def second_piece(base, row, first, second, whole, down):
        block, part = (row[-1], second) if down else (row[1], first)
        arrived(block, part, base + (1 if down else 3))
        to_sibling(block, whole)
        return block, part

    def far_piece(base, first, second, row, down):
        block, part = (row[2], first) if down else (row[2], second)
        arrived(block, part, base + (4 if down else 5))
        to_sibling(block, part)
        return block, part

    def b_first(down):
        block, part = first_piece(0, here, B0, B1, down)
        send(block, part, yn, 21 if down else 22)

    def b_second(down):
        second_piece(0, here, B0, B1, B, down)

    def b_second_across():
        send(here[-1], B1, yn, 23)
        send(here[1], B0, yn, 24)

    def b_far(down):
        block, part = far_piece(0, B0, B1, here, down)
        send(block, part, yn, 25 if down else 26)

    def a_across(n):
        part = (A0, A1)[n]
        arrived(there[0], part, 18 + n)
        if n == 0:
            send(there[0], A0, zp, 12)
            send(there[0], A0, zm, 15)
        else:
            send(there[0], A1, zm, 14)
            send(there[0], A1, zp, 13)
            to_sibling(there[0], A)

    def b_across(n):
        block, part = [
            (there[0], B), (there[-1], B0), (there[1], B1), (there[-1], B1), (there[1], B0), (there[2], B0), (there[2], B1)][n]
        arrived(block, part, 20 + n)
        to_sibling(block, part)

    along(0, here[0], B0, B1)
    send(here[0], A0, yn, 18)
    along_rest(0, here[0], B0, B1)
    send(here[0], A1, yn, 19)
    along(6, here[0], A0, A1)
    to_sibling(here[0], WHOLE)

    loads[3].wait()
    length = [len_s[s] for s in range(SESSIONS)]
    loads[4].wait()
    for s in range(SESSIONS):
        for t in range(STEPS):
            for q in range(GROUP):
                qrows[s, pl.ds(t * GROUP + q, 1), :] = qbuf[t, pl.ds(s, 1), pl.ds(q * HEAD_DIM, HEAD_DIM)].astype(F32)

    def score(s):
        loads[5 + s].wait()
        q = qrows[s].astype(BF16)

        def body(i, largest):
            start = pl.multiple_of(i * CHUNK, CHUNK)
            part = lax.dot_general(
                q, kbuf[s, pl.ds(start, CHUNK), :], (((1,), (1,)), ((), ())), preferred_element_type=F32) * SCALE
            slot = lax.broadcasted_iota(jnp.int32, (QROWS, CHUNK), 1) + start
            part = jnp.where(slot < length[s], part, -jnp.inf)
            scores[s, :, pl.ds(start, CHUNK)] = part
            for j in range(CHUNK // HEAD_DIM):
                largest = jnp.maximum(largest, part[:, j * HEAD_DIM : (j + 1) * HEAD_DIM])
            return largest

        largest = lax.fori_loop(0, SLOTS // CHUNK, body, jnp.full((QROWS, HEAD_DIM), -jnp.inf, F32))
        return jnp.max(largest, axis=1, keepdims=True)

    def weigh(s, top):
        loads[7 + s].wait()

        def body(i, carry):
            total, acc = carry
            start = pl.multiple_of(i * CHUNK, CHUNK)
            p = jnp.exp(scores[s, :, pl.ds(start, CHUNK)] - top)
            for j in range(CHUNK // HEAD_DIM):
                total = total + p[:, j * HEAD_DIM : (j + 1) * HEAD_DIM]
            acc = acc + jnp.dot(p.astype(BF16), vbuf[s, pl.ds(start, CHUNK), :], preferred_element_type=F32)
            return total, acc

        zero = jnp.zeros((QROWS, HEAD_DIM), F32)
        total, acc = lax.fori_loop(0, SLOTS // CHUNK, body, (zero, zero))
        return jnp.sum(total, axis=1, keepdims=True), acc

    top = [None, None]
    total = [None, None]
    acc = [None, None]
    top[0] = score(0)
    top[1] = score(1)

    pltpu.make_async_copy(hrecv.at[pl.ds(0, REPS - 1)], hrecv.at[pl.ds(0, REPS - 1)], small_recv.at[0]).wait()
    for r in range(REPS):
        for t in range(STEPS):
            hall[pl.ds(r * TOKENS + t * SESSIONS, SESSIONS), :] = hrecv[r, t].astype(F32)
    product = jnp.dot(hall[...].astype(BF16), pooled[rep], preferred_element_type=F32)
    for r in range(REPS):
        psend[r] = product[r * TOKENS : (r + 1) * TOKENS, :]

    @pl.loop(1, REPS)
    def _(k):
        peer = lax.rem(rep + k, REPS)
        small(psend.at[peer], precv.at[rep], 1, (peer, tp)).start()

    precv[rep] = psend[rep]

    along_rest(6, here[0], A0, A1)
    send(here[0], B, yn, 20)
    b_first(True)
    b_first(False)
    a_across(0)
    b_second(True)
    b_second(False)
    a_across(1)
    total[0], acc[0] = weigh(0, top[0])
    first_piece(6, here, A0, A1, True)
    first_piece(6, here, A0, A1, False)
    total[1], acc[1] = weigh(1, top[1])

    pltpu.make_async_copy(precv.at[pl.ds(0, REPS - 1)], precv.at[pl.ds(0, REPS - 1)], small_recv.at[1]).wait()
    projected = precv[0]
    for r in range(1, REPS):
        projected = projected + precv[r]
    row = lax.broadcasted_iota(jnp.int32, (TOKENS, HEAD_DIM), 0)
    lane = lax.broadcasted_iota(jnp.int32, (TOKENS, HEAD_DIM), 1)
    position = jnp.where(row % 2 == 0, length[0], length[1]) + row // 2
    angle = position.astype(F32) * frequencies((TOKENS, HEAD_DIM))
    raw = projected[:, :HEAD_DIM]
    swapped = jnp.concatenate([raw[:, HEAD_DIM // 2 :], raw[:, : HEAD_DIM // 2]], axis=1)
    sine = jnp.where(lane < HEAD_DIM // 2, -jnp.sin(angle), jnp.sin(angle))
    new_keys = (raw * jnp.cos(angle) + swapped * sine).astype(BF16)
    new_values = projected[:, HEAD_DIM:].astype(BF16)
    for t in range(STEPS):
        appended[t, :, pl.ds(0, HEAD_DIM)] = new_keys[t * SESSIONS : (t + 1) * SESSIONS, :]
        appended[t, :, pl.ds(HEAD_DIM, HEAD_DIM)] = new_values[t * SESSIONS : (t + 1) * SESSIONS, :]
    new_keys = new_keys.astype(F32)
    new_values = new_values.astype(F32)
    second = lax.broadcasted_iota(jnp.int32, (QROWS, 1), 0) >= GROUP
    for s in range(SESSIONS):
        q = qrows[s]
        fresh = [
            jnp.sum(q * new_keys[u * SESSIONS + s : u * SESSIONS + s + 1, :], axis=1, keepdims=True) * SCALE
            for u in range(STEPS)]
        fresh[1] = jnp.where(second, fresh[1], -jnp.inf)
        peak = jnp.maximum(top[s], jnp.maximum(fresh[0], fresh[1]))
        keep = jnp.exp(top[s] - peak)
        fresh = [jnp.exp(x - peak) for x in fresh]
        whole = total[s] * keep + fresh[0] + fresh[1]
        out = acc[s] * (keep / whole)
        for u in range(STEPS):
            out = out + (fresh[u] / whole).astype(BF16).astype(F32) * new_values[u * SESSIONS + s : u * SESSIONS + s + 1, :]
        heads[s] = out
    lhs[...] = jnp.zeros(lhs.shape, F32)
    for s in range(SESSIONS):
        for t in range(STEPS):
            for q in range(GROUP):
                lhs[pl.ds(t * SESSIONS + s, 1), pl.ds(q * HEAD_DIM, HEAD_DIM)] = heads[s, pl.ds(t * GROUP + q, 1), :]
    left = lhs[...].astype(BF16)
    loads[9].wait()

    @pl.when(rep != 1)
    def _():
        pl.semaphore_wait(ready, 1)

    @pl.when(rep == 1)
    def _():
        pl.semaphore_wait(barrier, TPS - 1)

        @pl.loop(0, REPS)
        def _(k):
            @pl.when(k != 1)
            def _():
                pl.semaphore_signal(ready, inc=1, device_id=(k, tp), device_id_type=MESH)

    for half in range(2):
        @pl.loop(0, HALF // OUT_COLS)
        def _(i):
            start = pl.multiple_of(i * OUT_COLS, OUT_COLS)
            part = jnp.dot(left, wbuf[:, pl.ds(half * HALF + start, OUT_COLS)], preferred_element_type=F32)
            osend[half, :, pl.ds(start, OUT_COLS)] = part[:TOKENS].astype(BF16)

        @pl.loop(1, TPS)
        def _(k):
            small(osend.at[half], orecv.at[half, tp], 2, (rep, lax.rem(tp + k, TPS))).start()

    b_second_across()
    second_piece(6, here, A0, A1, A, True)
    second_piece(6, here, A0, A1, A, False)
    b_across(0)
    b_far(True)
    b_far(False)
    b_across(1)
    b_across(2)
    first_piece(12, there, A0, A1, True)
    first_piece(12, there, A0, A1, False)
    b_across(3)
    second_piece(12, there, A0, A1, A, True)
    second_piece(12, there, A0, A1, A, False)
    b_across(4)
    far_piece(6, A0, A1, here, True)
    far_piece(6, A0, A1, here, False)
    b_across(5)
    b_across(6)
    far_piece(12, A0, A1, there, True)
    far_piece(12, A0, A1, there, False)

    def drain(ref, sem):
        pltpu.make_async_copy(ref, ref, sem).wait()

    others = orecv.at[:, pl.ds(0, TPS - 1)]
    drain(others, small_recv.at[2])
    for half in range(2):
        orecv[half, tp] = osend[half]
        for i in range(HALF // OUT_COLS):
            columns = pl.ds(i * OUT_COLS, OUT_COLS)
            summed = orecv[half, 0, :, columns].astype(F32)
            for r in range(1, TPS):
                summed = summed + orecv[half, r, :, columns].astype(F32)
            summed = summed.astype(BF16)
            for t in range(STEPS):
                attended[t, :, pl.ds(half * HALF + i * OUT_COLS, OUT_COLS)] = summed[t * SESSIONS : (t + 1) * SESSIONS, :]

    drain(pooled.at[pl.ds(0, REPS // 2)], sib_recv)
    drain(pooled.at[pl.ds(0, REPS - 1)], bulk_send)
    drain(hsend.at[pl.ds(0, REPS - 1)], small_send.at[0])
    drain(psend.at[pl.ds(0, REPS - 1)], small_send.at[1])
    drain(others, small_send.at[2])


def write_kernel(owners, pooled, attended, appended, installed, attended_out, appended_out, sem):
    copies = [
        pltpu.make_async_copy(pooled.at[owners[s]], installed.at[s], sem.at[s]) for s in range(REPS)]
    copies.append(pltpu.make_async_copy(attended, attended_out, sem.at[REPS]))
    copies.append(pltpu.make_async_copy(appended, appended_out, sem.at[REPS + 1]))
    for copy in copies:
        copy.start()
    for copy in copies:
        copy.wait()


def shards(hidden, queries, sectioned, owners, keys, values, lengths, weight):
    operands = [
        pltpu.with_memory_space_constraint(x, pltpu.HBM)
        for x in (hidden, queries, sectioned, owners, keys, values, lengths, weight)]
    hbm = pl.BlockSpec(memory_space=pltpu.HBM)
    vmem = pl.BlockSpec(memory_space=pltpu.VMEM)
    pooled, attended, appended = pl.pallas_call(
        main_kernel,
        out_shape=(
            pltpu.VMEM((REPS, ROWS, COLS), BF16),
            pltpu.VMEM((STEPS, SESSIONS, 2 * HALF), BF16),
            pltpu.VMEM((STEPS, SESSIONS, COLS), BF16),
        ),
        in_specs=[hbm] * 8,
        out_specs=(vmem, vmem, vmem),
        scratch_shapes=[
            pltpu.VMEM((SESSIONS, SLOTS, HEAD_DIM), BF16),
            pltpu.VMEM((SESSIONS, SLOTS, HEAD_DIM), BF16),
            pltpu.VMEM((GROUP * HEAD_DIM, 2 * HALF), BF16),
            pltpu.VMEM((STEPS, SESSIONS, REPS * ROWS), BF16),
            pltpu.VMEM((STEPS, SESSIONS, GROUP * HEAD_DIM), BF16),
            pltpu.SMEM((REPS,), jnp.int32),
            pltpu.SMEM((SESSIONS,), jnp.int32),
            pltpu.VMEM((REPS, STEPS, SESSIONS, ROWS), BF16),
            pltpu.VMEM((REPS, STEPS, SESSIONS, ROWS), BF16),
            pltpu.VMEM((REPS, STEPS, SESSIONS, ROWS), BF16),
            pltpu.VMEM((REPS * TOKENS, ROWS), F32),
            pltpu.VMEM((REPS, TOKENS, COLS), F32),
            pltpu.VMEM((REPS, TOKENS, COLS), F32),
            pltpu.VMEM((SESSIONS, QROWS, HEAD_DIM), F32),
            pltpu.VMEM((SESSIONS, QROWS, SLOTS), F32),
            pltpu.VMEM((SESSIONS, QROWS, HEAD_DIM), F32),
            pltpu.VMEM((8, GROUP * HEAD_DIM), F32),
            pltpu.VMEM((2, TOKENS, HALF), BF16),
            pltpu.VMEM((2, TPS, TOKENS, HALF), BF16),
            pltpu.SemaphoreType.DMA((10,)),
            pltpu.SemaphoreType.DMA,
            pltpu.SemaphoreType.DMA((27,)),
            pltpu.SemaphoreType.DMA,
            pltpu.SemaphoreType.DMA((3,)),
            pltpu.SemaphoreType.DMA((3,)),
            pltpu.SemaphoreType.REGULAR,
        ],
        compiler_params=pltpu.CompilerParams(
            collective_id=0, has_side_effects=True, vmem_limit_bytes=32 << 20),
        name="gather_and_attend",
    )(*operands)
    installed, attended, appended = pl.pallas_call(
        write_kernel,
        out_shape=(
            jax.ShapeDtypeStruct((REPS, ROWS, COLS), BF16),
            jax.ShapeDtypeStruct(attended.shape, BF16),
            jax.ShapeDtypeStruct(appended.shape, BF16),
        ),
        grid_spec=pltpu.PrefetchScalarGridSpec(
            num_scalar_prefetch=1,
            grid=(),
            in_specs=[vmem, vmem, vmem],
            out_specs=(hbm, hbm, hbm),
            scratch_shapes=[pltpu.SemaphoreType.DMA((REPS + 2,))],
        ),
        compiler_params=pltpu.CompilerParams(vmem_limit_bytes=4 << 20),
        name="write_in_order",
    )(owners, pooled, attended, appended)
    return installed.reshape(REPS * ROWS, COLS), appended, attended


def solution(mesh):
    in_specs = (
        P(None, "rep", None),
        P(None, "rep", "tp"),
        P("rep", "tp"),
        P(),
        P("rep", None, "tp"),
        P("rep", None, "tp"),
        P("rep"),
        P("tp", None),
    )
    out_specs = (P(None, "tp"), P(None, "rep", "tp"), P(None, "rep", None))
    return jax.shard_map(shards, mesh=mesh, in_specs=in_specs, out_specs=out_specs, check_vma=False)
```

time: 44.6 us -> 31.3 us (0.70)
  the two profiles are of different devices: /device:TPU:0 before, /device:TPU:1 now
where the time goes in v2:
time: 31.3 us; the launch traced here: 31.2 us
  Pallas kernels  30.5 us (97%)
  between operations  0.66 us (2%)
    pallas_call x1, Pallas kernels, shards(): pl.pallas_call(main_kernel, out_shape=(pltpu.VMEM((REPS, ROWS, COLS), BF1...  27.8 us
    pallas_call x1, Pallas kernels, shards(): pl.pallas_call(write_kernel, out_shape=(jax.ShapeDtypeStruct((REPS, ROWS,...  2.7 us

profile of v2, /device:TPU:1, one launch (start us, length us, event | category | flops | bytes accessed | tf_op | source)
XLA Modules:
  0.0 31.2 jit_solution(16352711267718036487)
XLA Ops:
  0.6 0.0 copy-start
  0.6 27.8 %gather_and_attend.1 = (bf16[16,512,256]{2,1,0:T(8,128)(2,1)S(1)}, bf16[2,2,4096]{2,1,0:T(2,128)(2,1)S(1)}, bf16[2,2,256]{2,1,0:T(2,128)(2,1)S(1)}) custom-call(bf16[2,2,8192]{2,1,0:T(2,128)(2,1)} %hidden.1, bf16[2,2,1024]{2,1,0:T(2,128)(2,1)} %queries.1, bf16[512,256]{1,0:T(8,128)(2,1)} %sectioned.1, s32[16]{0:T(128)} %owners.3, ...), custom_call_target="tpu_custom_call" | custom-call | tf_op jit(solution)/shard_map/gather_and_attend/pallas_call | solution.py:430
  28.5 0.0 copy-done
  28.5 2.7 %write_in_order.1 = (bf16[16,512,256]{2,1,0:T(8,128)(2,1)}, bf16[2,2,4096]{2,1,0:T(2,128)(2,1)}, bf16[2,2,256]{2,1,0:T(2,128)(2,1)}) custom-call(s32[16]{0:T(128)S(1)} %copy-done, bf16[16,512,256]{2,1,0:T(8,128)(2,1)S(1)} %get-tuple-element.9.pooled, bf16[2,2,4096]{2,1,0:T(2,128)(2,1)S(1)} %get-tuple-element.10.attended, ...), custom_call_target="tpu_custom_call" | custom-call | tf_op jit(solution)/shard_map/write_in_order/pallas_call | solution.py:471
Async XLA Ops:
  0.6 27.9 %copy-start = (s32[16]{0:T(128)S(1)}, s32[16]{0:T(128)}, u32[]{:S(2)}) copy-start(s32[16]{0:T(128)} %owners.3) | copy-start | bytes 196

commit v3 on v2

--- a/solution.py
+++ b/solution.py
@@ -159,69 +159,46 @@
     there = {
         0: chip(1 - y, z, c), 1: chip(1 - y, z + 1, c), -1: chip(1 - y, z - 1, c), 2: chip(1 - y, z + 2, c)}
 
-    def along(base, block, first, second):
-        send(block, first, zp, base)
-        send(block, second, zm, base + 2)
-
-    def along_rest(base, block, first, second):
-        send(block, second, zp, base + 1)
-        send(block, first, zm, base + 3)
-
-    def first_piece(base, row, first, second, down):
-        block, part = (row[-1], first) if down else (row[1], second)
-        arrived(block, part, base if down else base + 2)
-        send(block, part, zp if down else zm, base + (4 if down else 5))
-        return block, part
-
-    def second_piece(base, row, first, second, whole, down):
-        block, part = (row[-1], second) if down else (row[1], first)
-        arrived(block, part, base + (1 if down else 3))
-        to_sibling(block, whole)
-        return block, part
-
-    def far_piece(base, first, second, row, down):
-        block, part = (row[2], first) if down else (row[2], second)
-        arrived(block, part, base + (4 if down else 5))
-        to_sibling(block, part)
-        return block, part
-
-    def b_first(down):
-        block, part = first_piece(0, here, B0, B1, down)
-        send(block, part, yn, 21 if down else 22)
-
-    def b_second(down):
-        second_piece(0, here, B0, B1, B, down)
-
-    def b_second_across():
-        send(here[-1], B1, yn, 23)
-        send(here[1], B0, yn, 24)
-
-    def b_far(down):
-        block, part = far_piece(0, B0, B1, here, down)
-        send(block, part, yn, 25 if down else 26)
-
-    def a_across(n):
-        part = (A0, A1)[n]
-        arrived(there[0], part, 18 + n)
-        if n == 0:
-            send(there[0], A0, zp, 12)
-            send(there[0], A0, zm, 15)
+    route = [
+        (here[-1], B, [(zp, B0, 5), (yn, B, 7)]),
+        (here[1], B, [(zm, B1, 6), (yn, B, 8)]),
+        (there[0], A, [(zp, A, 11), (zm, A, 12)]),
+        (here[-1], A, [(zp, A0, 13)]),
+        (here[1], A, [(zm, A1, 14)]),
+        (here[2], B0, [(yn, B0, 9)]),
+        (here[2], B1, [(yn, B1, 10)]),
+        (there[-1], B, []),
+        (there[1], B, []),
+        (there[2], B0, []),
+        (there[2], B1, []),
+        (there[-1], A, [(zp, A0, 15)]),
+        (there[1], A, [(zm, A1, 16)]),
+        (here[2], A0, []),
+        (here[2], A1, []),
+        (there[2], A0, []),
+        (there[2], A1, []),
+        (there[0], B, []),
+    ]
+
+    def events(*slots):
+        for n in slots:
+            block, part, onward = route[n]
+            arrived(block, part, n)
+            for device, onward_part, slot in onward:
+                send(block, onward_part, device, slot)
+        done = [(route[n][0], route[n][1]) for n in slots]
+        if len(done) == 2 and done[0][0] is done[1][0]:
+            to_sibling(done[0][0], (done[0][1][0], done[0][1][1] + done[1][1][1]))
         else:
-            send(there[0], A1, zm, 14)
-            send(there[0], A1, zp, 13)
-            to_sibling(there[0], A)
-
-    def b_across(n):
-        block, part = [
-            (there[0], B), (there[-1], B0), (there[1], B1), (there[-1], B1), (there[1], B0), (there[2], B0), (there[2], B1)][n]
-        arrived(block, part, 20 + n)
-        to_sibling(block, part)
-
-    along(0, here[0], B0, B1)
-    send(here[0], A0, yn, 18)
-    along_rest(0, here[0], B0, B1)
-    send(here[0], A1, yn, 19)
-    along(6, here[0], A0, A1)
+            for block, part in done:
+                to_sibling(block, part)
+
+    send(here[0], B, zp, 0)
+    send(here[0], B, zm, 1)
+    send(here[0], A, yn, 2)
+    send(here[0], A, zp, 3)
+    send(here[0], A, zm, 4)
+    send(here[0], B, yn, 17)
     to_sibling(here[0], WHOLE)
 
     loads[3].wait()
@@ -287,18 +264,12 @@
 
     precv[rep] = psend[rep]
 
-    along_rest(6, here[0], A0, A1)
-    send(here[0], B, yn, 20)
-    b_first(True)
-    b_first(False)
-    a_across(0)
-    b_second(True)
-    b_second(False)
-    a_across(1)
+    events(0, 1)
+    events(2)
     total[0], acc[0] = weigh(0, top[0])
-    first_piece(6, here, A0, A1, True)
-    first_piece(6, here, A0, A1, False)
     total[1], acc[1] = weigh(1, top[1])
+    events(3, 4)
+    events(5, 6)
 
     pltpu.make_async_copy(precv.at[pl.ds(0, REPS - 1)], precv.at[pl.ds(0, REPS - 1)], small_recv.at[1]).wait()
     projected = precv[0]
@@ -366,26 +337,12 @@
         def _(k):
             small(osend.at[half], orecv.at[half, tp], 2, (rep, lax.rem(tp + k, TPS))).start()
 
-    b_second_across()
-    second_piece(6, here, A0, A1, A, True)
-    second_piece(6, here, A0, A1, A, False)
-    b_across(0)
-    b_far(True)
-    b_far(False)
-    b_across(1)
-    b_across(2)
-    first_piece(12, there, A0, A1, True)
-    first_piece(12, there, A0, A1, False)
-    b_across(3)
-    second_piece(12, there, A0, A1, A, True)
-    second_piece(12, there, A0, A1, A, False)
-    b_across(4)
-    far_piece(6, A0, A1, here, True)
-    far_piece(6, A0, A1, here, False)
-    b_across(5)
-    b_across(6)
-    far_piece(12, A0, A1, there, True)
-    far_piece(12, A0, A1, there, False)
+    events(11, 12)
+    events(17)
+    events(7, 8)
+    events(13, 14)
+    events(9, 10)
+    events(15, 16)
 
     def drain(ref, sem):
         pltpu.make_async_copy(ref, ref, sem).wait()
@@ -458,7 +415,7 @@
             pltpu.VMEM((2, TPS, TOKENS, HALF), BF16),
             pltpu.SemaphoreType.DMA((10,)),
             pltpu.SemaphoreType.DMA,
-            pltpu.SemaphoreType.DMA((27,)),
+            pltpu.SemaphoreType.DMA((18,)),
             pltpu.SemaphoreType.DMA,
             pltpu.SemaphoreType.DMA((3,)),
             pltpu.SemaphoreType.DMA((3,)),

time: 31.3 us -> 29.7 us (0.949)
  the two profiles are of different devices: /device:TPU:1 before, /device:TPU:0 now
where the time goes in v3:
time: 29.7 us; the launch traced here: 29.2 us
  Pallas kernels  28.6 us (96%)
  between operations  0.66 us (2%)
    pallas_call x1, Pallas kernels, shards(): pl.pallas_call(main_kernel, out_shape=(pltpu.VMEM((REPS, ROWS, COLS), BF1...  25.9 us
    pallas_call x1, Pallas kernels, shards(): pl.pallas_call(write_kernel, out_shape=(jax.ShapeDtypeStruct((REPS, ROWS,...  2.7 us

profile of v3, /device:TPU:0, one launch (start us, length us, event | category | flops | bytes accessed | tf_op | source)
XLA Modules:
  0.0 29.2 jit_solution(7176929465498856040)
XLA Ops:
  0.6 0.0 copy-start
  0.6 25.9 %gather_and_attend.1 = (bf16[16,512,256]{2,1,0:T(8,128)(2,1)S(1)}, bf16[2,2,4096]{2,1,0:T(2,128)(2,1)S(1)}, bf16[2,2,256]{2,1,0:T(2,128)(2,1)S(1)}) custom-call(bf16[2,2,8192]{2,1,0:T(2,128)(2,1)} %hidden.1, bf16[2,2,1024]{2,1,0:T(2,128)(2,1)} %queries.1, bf16[512,256]{1,0:T(8,128)(2,1)} %sectioned.1, s32[16]{0:T(128)} %owners.3, ...), custom_call_target="tpu_custom_call" | custom-call | tf_op jit(solution)/shard_map/gather_and_attend/pallas_call | solution.py:387
  26.5 0.0 copy-done
  26.5 2.7 %write_in_order.1 = (bf16[16,512,256]{2,1,0:T(8,128)(2,1)}, bf16[2,2,4096]{2,1,0:T(2,128)(2,1)}, bf16[2,2,256]{2,1,0:T(2,128)(2,1)}) custom-call(s32[16]{0:T(128)S(1)} %copy-done, bf16[16,512,256]{2,1,0:T(8,128)(2,1)S(1)} %get-tuple-element.9.pooled, bf16[2,2,4096]{2,1,0:T(2,128)(2,1)S(1)} %get-tuple-element.10.attended, ...), custom_call_target="tpu_custom_call" | custom-call | tf_op jit(solution)/shard_map/write_in_order/pallas_call | solution.py:428
Async XLA Ops:
  0.6 25.9 %copy-start = (s32[16]{0:T(128)S(1)}, s32[16]{0:T(128)}, u32[]{:S(2)}) copy-start(s32[16]{0:T(128)} %owners.3) | copy-start | bytes 196

commit v4 on v3

--- a/solution.py
+++ b/solution.py
@@ -27,14 +27,17 @@
 SLOTS = 8192
 CHUNK = 2048
 OUT_COLS = 512
-HALF = 2048
-
-A0 = (0, 160)
-A1 = (160, 176)
-A = (0, 336)
-B0 = (336, 80)
-B1 = (416, 96)
-B = (336, 176)
+PARTS = 4
+PART = 1024
+
+A0 = (0, 176)
+A1 = (176, 176)
+A = (0, 352)
+B0 = (352, 80)
+B1 = (432, 80)
+B = (352, 160)
+A0_MOST, A0_END = (0, 112), (112, 64)
+A1_MOST, A1_END = (176, 112), (288, 64)
 WHOLE = (0, 512)
 
 
@@ -65,6 +68,9 @@
     zm = (chip(y, z - 1, c), tp)
     yn = (chip(1 - y, z, c), tp)
     sib = (chip(y, z, 1 - c), tp)
+    zp_other = (chip(y, z + 1, 1 - c), tp)
+    zm_other = (chip(y, z - 1, 1 - c), tp)
+    far_other = chip(1 - y, z + 2, 1 - c)
 
     loads = [
         pltpu.make_async_copy(owners, own_s, load_sem.at[0]),
@@ -89,18 +95,16 @@
         def _():
             pl.semaphore_signal(barrier, inc=1, device_id=(k, tp), device_id_type=MESH)
 
-    loads[0].wait()
-
     loads[1].wait()
     for r in range(REPS):
         for t in range(STEPS):
             hsplit[r, t] = hbuf[t, :, pl.ds(r * ROWS, ROWS)]
-
-    @pl.loop(0, REPS)
-    def _(r):
+    loads[0].wait()
+    owner = [own_s[s] for s in range(REPS)]
+    for r in range(REPS):
         found = jnp.int32(0)
         for s in range(1, REPS):
-            found = jnp.where(own_s[s] == r, s, found)
+            found = jnp.where(owner[s] == r, s, found)
         hsend[r] = hsplit[found]
 
     loads[2].wait()
@@ -114,10 +118,6 @@
     @pl.when(rep == 0)
     def _():
         pl.semaphore_signal(ready, inc=1, device_id=(1, tp), device_id_type=MESH)
-
-        @pl.loop(1, TPS)
-        def _(k):
-            pl.semaphore_signal(barrier, inc=1, device_id=(1, lax.rem(tp + k, TPS)), device_id_type=MESH)
 
     @pl.when(rep == 1)
     def _():
@@ -171,12 +171,12 @@
         (there[1], B, []),
         (there[2], B0, []),
         (there[2], B1, []),
-        (there[-1], A, [(zp, A0, 15)]),
-        (there[1], A, [(zm, A1, 16)]),
+        (there[-1], A, [(zp, A0_MOST, 15), (zp, A0_END, 18), (zp_other, A0_END, 19)]),
+        (there[1], A, [(zm, A1_MOST, 16), (zm, A1_END, 20), (zm_other, A1_END, 21)]),
         (here[2], A0, []),
         (here[2], A1, []),
-        (there[2], A0, []),
-        (there[2], A1, []),
+        (there[2], A0_MOST, []),
+        (there[2], A1_MOST, []),
         (there[0], B, []),
     ]
 
@@ -187,7 +187,7 @@
             for device, onward_part, slot in onward:
                 send(block, onward_part, device, slot)
         done = [(route[n][0], route[n][1]) for n in slots]
-        if len(done) == 2 and done[0][0] is done[1][0]:
+        if len(done) == 2 and done[0][0] is done[1][0] and sum(done[0][1]) == done[1][1][0]:
             to_sibling(done[0][0], (done[0][1][0], done[0][1][1] + done[1][1][1]))
         else:
             for block, part in done:
@@ -200,6 +200,12 @@
     send(here[0], A, zm, 4)
     send(here[0], B, yn, 17)
     to_sibling(here[0], WHOLE)
+
+    @pl.when(rep == 0)
+    def _():
+        @pl.loop(1, TPS)
+        def _(k):
+            pl.semaphore_signal(barrier, inc=1, device_id=(1, lax.rem(tp + k, TPS)), device_id_type=MESH)
 
     loads[3].wait()
     length = [len_s[s] for s in range(SESSIONS)]
@@ -255,7 +261,7 @@
             hall[pl.ds(r * TOKENS + t * SESSIONS, SESSIONS), :] = hrecv[r, t].astype(F32)
     product = jnp.dot(hall[...].astype(BF16), pooled[rep], preferred_element_type=F32)
     for r in range(REPS):
-        psend[r] = product[r * TOKENS : (r + 1) * TOKENS, :]
+        psend[r] = product[r * TOKENS : (r + 1) * TOKENS, :].astype(BF16)
 
     @pl.loop(1, REPS)
     def _(k):
@@ -269,20 +275,26 @@
     total[0], acc[0] = weigh(0, top[0])
     total[1], acc[1] = weigh(1, top[1])
     events(3, 4)
-    events(5, 6)
-
-    pltpu.make_async_copy(precv.at[pl.ds(0, REPS - 1)], precv.at[pl.ds(0, REPS - 1)], small_recv.at[1]).wait()
-    projected = precv[0]
-    for r in range(1, REPS):
-        projected = projected + precv[r]
+
+    @pl.when(tp < TPS // 2)
+    def _():
+        events(5, 6)
+
     row = lax.broadcasted_iota(jnp.int32, (TOKENS, HEAD_DIM), 0)
     lane = lax.broadcasted_iota(jnp.int32, (TOKENS, HEAD_DIM), 1)
     position = jnp.where(row % 2 == 0, length[0], length[1]) + row // 2
     angle = position.astype(F32) * frequencies((TOKENS, HEAD_DIM))
+    cosine = jnp.cos(angle)
+    sine = jnp.where(lane < HEAD_DIM // 2, -jnp.sin(angle), jnp.sin(angle))
+    lhs[...] = jnp.zeros(lhs.shape, F32)
+
+    pltpu.make_async_copy(precv.at[pl.ds(0, REPS - 1)], precv.at[pl.ds(0, REPS - 1)], small_recv.at[1]).wait()
+    projected = precv[0].astype(F32)
+    for r in range(1, REPS):
+        projected = projected + precv[r].astype(F32)
     raw = projected[:, :HEAD_DIM]
     swapped = jnp.concatenate([raw[:, HEAD_DIM // 2 :], raw[:, : HEAD_DIM // 2]], axis=1)
-    sine = jnp.where(lane < HEAD_DIM // 2, -jnp.sin(angle), jnp.sin(angle))
-    new_keys = (raw * jnp.cos(angle) + swapped * sine).astype(BF16)
+    new_keys = (raw * cosine + swapped * sine).astype(BF16)
     new_values = projected[:, HEAD_DIM:].astype(BF16)
     for t in range(STEPS):
         appended[t, :, pl.ds(0, HEAD_DIM)] = new_keys[t * SESSIONS : (t + 1) * SESSIONS, :]
@@ -304,7 +316,6 @@
         for u in range(STEPS):
             out = out + (fresh[u] / whole).astype(BF16).astype(F32) * new_values[u * SESSIONS + s : u * SESSIONS + s + 1, :]
         heads[s] = out
-    lhs[...] = jnp.zeros(lhs.shape, F32)
     for s in range(SESSIONS):
         for t in range(STEPS):
             for q in range(GROUP):
@@ -326,16 +337,20 @@
             def _():
                 pl.semaphore_signal(ready, inc=1, device_id=(k, tp), device_id_type=MESH)
 
-    for half in range(2):
-        @pl.loop(0, HALF // OUT_COLS)
+    for part in range(PARTS):
+        @pl.loop(0, PART // OUT_COLS)
         def _(i):
             start = pl.multiple_of(i * OUT_COLS, OUT_COLS)
-            part = jnp.dot(left, wbuf[:, pl.ds(half * HALF + start, OUT_COLS)], preferred_element_type=F32)
-            osend[half, :, pl.ds(start, OUT_COLS)] = part[:TOKENS].astype(BF16)
+            result = jnp.dot(left, wbuf[:, pl.ds(part * PART + start, OUT_COLS)], preferred_element_type=F32)
+            osend[part, :, pl.ds(start, OUT_COLS)] = result[:TOKENS].astype(BF16)
 
         @pl.loop(1, TPS)
         def _(k):
-            small(osend.at[half], orecv.at[half, tp], 2, (rep, lax.rem(tp + k, TPS))).start()
+            small(osend.at[part], orecv.at[part, tp], 2, (rep, lax.rem(tp + k, TPS))).start()
+
+    @pl.when(tp >= TPS // 2)
+    def _():
+        events(5, 6)
 
     events(11, 12)
     events(17)
@@ -347,20 +362,23 @@
     def drain(ref, sem):
         pltpu.make_async_copy(ref, ref, sem).wait()
 
+    arrived(there[2], A0_END, 18)
+    arrived(far_other, A0_END, 19)
+    arrived(there[2], A1_END, 20)
+    arrived(far_other, A1_END, 21)
     others = orecv.at[:, pl.ds(0, TPS - 1)]
     drain(others, small_recv.at[2])
-    for half in range(2):
-        orecv[half, tp] = osend[half]
-        for i in range(HALF // OUT_COLS):
+    for part in range(PARTS):
+        orecv[part, tp] = osend[part]
+        for i in range(PART // OUT_COLS):
             columns = pl.ds(i * OUT_COLS, OUT_COLS)
-            summed = orecv[half, 0, :, columns].astype(F32)
+            summed = orecv[part, 0, :, columns].astype(F32)
             for r in range(1, TPS):
-                summed = summed + orecv[half, r, :, columns].astype(F32)
+                summed = summed + orecv[part, r, :, columns].astype(F32)
             summed = summed.astype(BF16)
             for t in range(STEPS):
-                attended[t, :, pl.ds(half * HALF + i * OUT_COLS, OUT_COLS)] = summed[t * SESSIONS : (t + 1) * SESSIONS, :]
-
-    drain(pooled.at[pl.ds(0, REPS // 2)], sib_recv)
+                attended[t, :, pl.ds(part * PART + i * OUT_COLS, OUT_COLS)] = summed[t * SESSIONS : (t + 1) * SESSIONS, :]
+    drain(pooled.at[pl.ds(0, REPS // 2), pl.ds(0, ROWS - 16)], sib_recv)
     drain(pooled.at[pl.ds(0, REPS - 1)], bulk_send)
     drain(hsend.at[pl.ds(0, REPS - 1)], small_send.at[0])
     drain(psend.at[pl.ds(0, REPS - 1)], small_send.at[1])
@@ -388,7 +406,7 @@
         main_kernel,
         out_shape=(
             pltpu.VMEM((REPS, ROWS, COLS), BF16),
-            pltpu.VMEM((STEPS, SESSIONS, 2 * HALF), BF16),
+            pltpu.VMEM((STEPS, SESSIONS, PARTS * PART), BF16),
             pltpu.VMEM((STEPS, SESSIONS, COLS), BF16),
         ),
         in_specs=[hbm] * 8,
@@ -396,7 +414,7 @@
         scratch_shapes=[
             pltpu.VMEM((SESSIONS, SLOTS, HEAD_DIM), BF16),
             pltpu.VMEM((SESSIONS, SLOTS, HEAD_DIM), BF16),
-            pltpu.VMEM((GROUP * HEAD_DIM, 2 * HALF), BF16),
+            pltpu.VMEM((GROUP * HEAD_DIM, PARTS * PART), BF16),
             pltpu.VMEM((STEPS, SESSIONS, REPS * ROWS), BF16),
             pltpu.VMEM((STEPS, SESSIONS, GROUP * HEAD_DIM), BF16),
             pltpu.SMEM((REPS,), jnp.int32),
@@ -405,17 +423,17 @@
             pltpu.VMEM((REPS, STEPS, SESSIONS, ROWS), BF16),
             pltpu.VMEM((REPS, STEPS, SESSIONS, ROWS), BF16),
             pltpu.VMEM((REPS * TOKENS, ROWS), F32),
-            pltpu.VMEM((REPS, TOKENS, COLS), F32),
-            pltpu.VMEM((REPS, TOKENS, COLS), F32),
+            pltpu.VMEM((REPS, TOKENS, COLS), BF16),
+            pltpu.VMEM((REPS, TOKENS, COLS), BF16),
             pltpu.VMEM((SESSIONS, QROWS, HEAD_DIM), F32),
             pltpu.VMEM((SESSIONS, QROWS, SLOTS), F32),
             pltpu.VMEM((SESSIONS, QROWS, HEAD_DIM), F32),
             pltpu.VMEM((8, GROUP * HEAD_DIM), F32),
-            pltpu.VMEM((2, TOKENS, HALF), BF16),
-            pltpu.VMEM((2, TPS, TOKENS, HALF), BF16),
+            pltpu.VMEM((PARTS, TOKENS, PART), BF16),
+            pltpu.VMEM((PARTS, TPS, TOKENS, PART), BF16),
             pltpu.SemaphoreType.DMA((10,)),
             pltpu.SemaphoreType.DMA,
-            pltpu.SemaphoreType.DMA((18,)),
+            pltpu.SemaphoreType.DMA((22,)),
             pltpu.SemaphoreType.DMA,
             pltpu.SemaphoreType.DMA((3,)),
             pltpu.SemaphoreType.DMA((3,)),

time: 29.7 us -> 29.3 us (0.987)
  Pallas kernels: 28.6 us -> 28.1 us
    pallas_call x1, Pallas kernels: 25.9 us -> 25.4 us  [shards(): pl.pallas_call(main_kernel, out_shape=(pltpu.VMEM((REPS, ROWS, COLS), BF1...]
where the time goes in v4:
time: 29.3 us; the launch traced here: 28.7 us
  Pallas kernels  28.1 us (96%)
  between operations  0.66 us (2%)
    pallas_call x1, Pallas kernels, shards(): pl.pallas_call(main_kernel, out_shape=(pltpu.VMEM((REPS, ROWS, COLS), BF1...  25.4 us
    pallas_call x1, Pallas kernels, shards(): pl.pallas_call(write_kernel, out_shape=(jax.ShapeDtypeStruct((REPS, ROWS,...  2.7 us

profile of v4, /device:TPU:0, one launch (start us, length us, event | category | flops | bytes accessed | tf_op | source)
XLA Modules:
  0.0 28.7 jit_solution(1675882702897794169)
XLA Ops:
  0.6 0.0 copy-start
  0.6 25.4 %gather_and_attend.1 = (bf16[16,512,256]{2,1,0:T(8,128)(2,1)S(1)}, bf16[2,2,4096]{2,1,0:T(2,128)(2,1)S(1)}, bf16[2,2,256]{2,1,0:T(2,128)(2,1)S(1)}) custom-call(bf16[2,2,8192]{2,1,0:T(2,128)(2,1)} %hidden.1, bf16[2,2,1024]{2,1,0:T(2,128)(2,1)} %queries.1, bf16[512,256]{1,0:T(8,128)(2,1)} %sectioned.1, s32[16]{0:T(128)} %owners.3, ...), custom_call_target="tpu_custom_call" | custom-call | tf_op jit(solution)/shard_map/gather_and_attend/pallas_call | solution.py:405
  26.0 0.0 copy-done
  26.0 2.7 %write_in_order.1 = (bf16[16,512,256]{2,1,0:T(8,128)(2,1)}, bf16[2,2,4096]{2,1,0:T(2,128)(2,1)}, bf16[2,2,256]{2,1,0:T(2,128)(2,1)}) custom-call(s32[16]{0:T(128)S(1)} %copy-done, bf16[16,512,256]{2,1,0:T(8,128)(2,1)S(1)} %get-tuple-element.9.pooled, bf16[2,2,4096]{2,1,0:T(2,128)(2,1)S(1)} %get-tuple-element.10.attended, ...), custom_call_target="tpu_custom_call" | custom-call | tf_op jit(solution)/shard_map/write_in_order/pallas_call | solution.py:446
Async XLA Ops:
  0.6 25.4 %copy-start = (s32[16]{0:T(128)S(1)}, s32[16]{0:T(128)}, u32[]{:S(2)}) copy-start(s32[16]{0:T(128)} %owners.3) | copy-start | bytes 196

commit v5 on v4

--- a/solution.py
+++ b/solution.py
@@ -16,6 +16,8 @@
 BF16 = jnp.bfloat16
 
 REPS = 16
+HERALD = 2
+COLLECTOR = 3
 TPS = 8
 ROWS = 512
 COLS = 256
@@ -30,14 +32,14 @@
 PARTS = 4
 PART = 1024
 
-A0 = (0, 176)
-A1 = (176, 176)
-A = (0, 352)
-B0 = (352, 80)
-B1 = (432, 80)
-B = (352, 160)
-A0_MOST, A0_END = (0, 112), (112, 64)
-A1_MOST, A1_END = (176, 112), (288, 64)
+A0 = (0, 160)
+A1 = (160, 176)
+A = (0, 336)
+B0 = (336, 80)
+B1 = (416, 96)
+B = (336, 176)
+A0_MOST, A0_END = (0, 96), (96, 64)
+A1_MOST, A1_END = (160, 112), (272, 64)
 WHOLE = (0, 512)
 
 
@@ -91,7 +93,7 @@
 
     @pl.loop(0, REPS)
     def _(k):
-        @pl.when((k != rep) & (k != 1))
+        @pl.when((k != rep) & (k != COLLECTOR))
         def _():
             pl.semaphore_signal(barrier, inc=1, device_id=(k, tp), device_id_type=MESH)
 
@@ -111,15 +113,15 @@
     for load in loads[5:]:
         load.start()
 
-    @pl.when(rep != 1)
+    @pl.when(rep != COLLECTOR)
     def _():
         pl.semaphore_wait(barrier, REPS - 1)
 
-    @pl.when(rep == 0)
-    def _():
-        pl.semaphore_signal(ready, inc=1, device_id=(1, tp), device_id_type=MESH)
-
-    @pl.when(rep == 1)
+    @pl.when(rep == HERALD)
+    def _():
+        pl.semaphore_signal(ready, inc=1, device_id=(COLLECTOR, tp), device_id_type=MESH)
+
+    @pl.when(rep == COLLECTOR)
     def _():
         pl.semaphore_wait(ready, 1)
 
@@ -201,11 +203,11 @@
     send(here[0], B, yn, 17)
     to_sibling(here[0], WHOLE)
 
-    @pl.when(rep == 0)
+    @pl.when(rep == HERALD)
     def _():
         @pl.loop(1, TPS)
         def _(k):
-            pl.semaphore_signal(barrier, inc=1, device_id=(1, lax.rem(tp + k, TPS)), device_id_type=MESH)
+            pl.semaphore_signal(barrier, inc=1, device_id=(COLLECTOR, lax.rem(tp + k, TPS)), device_id_type=MESH)
 
     loads[3].wait()
     length = [len_s[s] for s in range(SESSIONS)]
@@ -276,9 +278,6 @@
     total[1], acc[1] = weigh(1, top[1])
     events(3, 4)
 
-    @pl.when(tp < TPS // 2)
-    def _():
-        events(5, 6)
 
     row = lax.broadcasted_iota(jnp.int32, (TOKENS, HEAD_DIM), 0)
     lane = lax.broadcasted_iota(jnp.int32, (TOKENS, HEAD_DIM), 1)
@@ -287,6 +286,16 @@
     cosine = jnp.cos(angle)
     sine = jnp.where(lane < HEAD_DIM // 2, -jnp.sin(angle), jnp.sin(angle))
     lhs[...] = jnp.zeros(lhs.shape, F32)
+
+    @pl.when(rep == COLLECTOR)
+    def _():
+        pl.semaphore_wait(barrier, TPS - 1)
+
+        @pl.loop(0, REPS)
+        def _(k):
+            @pl.when(k != COLLECTOR)
+            def _():
+                pl.semaphore_signal(ready, inc=1, device_id=(k, tp), device_id_type=MESH)
 
     pltpu.make_async_copy(precv.at[pl.ds(0, REPS - 1)], precv.at[pl.ds(0, REPS - 1)], small_recv.at[1]).wait()
     projected = precv[0].astype(F32)
@@ -320,22 +329,13 @@
         for t in range(STEPS):
             for q in range(GROUP):
                 lhs[pl.ds(t * SESSIONS + s, 1), pl.ds(q * HEAD_DIM, HEAD_DIM)] = heads[s, pl.ds(t * GROUP + q, 1), :]
+    events(5, 6)
     left = lhs[...].astype(BF16)
     loads[9].wait()
 
-    @pl.when(rep != 1)
+    @pl.when(rep != COLLECTOR)
     def _():
         pl.semaphore_wait(ready, 1)
-
-    @pl.when(rep == 1)
-    def _():
-        pl.semaphore_wait(barrier, TPS - 1)
-
-        @pl.loop(0, REPS)
-        def _(k):
-            @pl.when(k != 1)
-            def _():
-                pl.semaphore_signal(ready, inc=1, device_id=(k, tp), device_id_type=MESH)
 
     for part in range(PARTS):
         @pl.loop(0, PART // OUT_COLS)
@@ -347,10 +347,6 @@
         @pl.loop(1, TPS)
         def _(k):
             small(osend.at[part], orecv.at[part, tp], 2, (rep, lax.rem(tp + k, TPS))).start()
-
-    @pl.when(tp >= TPS // 2)
-    def _():
-        events(5, 6)
 
     events(11, 12)
     events(17)

time: 29.3 us -> 28.7 us (0.980); the launches traced: 28.7 us -> 28.5 us
  no operation moved by 1% of the time
where the time goes in v5:
time: 28.7 us; the launch traced here: 28.5 us
  Pallas kernels  27.9 us (97%)
  between operations  0.66 us (2%)
    pallas_call x1, Pallas kernels, shards(): pl.pallas_call(main_kernel, out_shape=(pltpu.VMEM((REPS, ROWS, COLS), BF1...  25.2 us
    pallas_call x1, Pallas kernels, shards(): pl.pallas_call(write_kernel, out_shape=(jax.ShapeDtypeStruct((REPS, ROWS,...  2.7 us

profile of v5, /device:TPU:0, one launch (start us, length us, event | category | flops | bytes accessed | tf_op | source)
XLA Modules:
  0.0 28.5 jit_solution(9886971584618415839)
XLA Ops:
  0.6 0.0 copy-start
  0.6 25.2 %gather_and_attend.1 = (bf16[16,512,256]{2,1,0:T(8,128)(2,1)S(1)}, bf16[2,2,4096]{2,1,0:T(2,128)(2,1)S(1)}, bf16[2,2,256]{2,1,0:T(2,128)(2,1)S(1)}) custom-call(bf16[2,2,8192]{2,1,0:T(2,128)(2,1)} %hidden.1, bf16[2,2,1024]{2,1,0:T(2,128)(2,1)} %queries.1, bf16[512,256]{1,0:T(8,128)(2,1)} %sectioned.1, s32[16]{0:T(128)} %owners.3, ...), custom_call_target="tpu_custom_call" | custom-call | tf_op jit(solution)/shard_map/gather_and_attend/pallas_call | solution.py:401
  25.8 0.0 copy-done
  25.8 2.7 %write_in_order.1 = (bf16[16,512,256]{2,1,0:T(8,128)(2,1)}, bf16[2,2,4096]{2,1,0:T(2,128)(2,1)}, bf16[2,2,256]{2,1,0:T(2,128)(2,1)}) custom-call(s32[16]{0:T(128)S(1)} %copy-done, bf16[16,512,256]{2,1,0:T(8,128)(2,1)S(1)} %get-tuple-element.9.pooled, bf16[2,2,4096]{2,1,0:T(2,128)(2,1)S(1)} %get-tuple-element.10.attended, ...), custom_call_target="tpu_custom_call" | custom-call | tf_op jit(solution)/shard_map/write_in_order/pallas_call | solution.py:442
Async XLA Ops:
  0.6 25.2 %copy-start = (s32[16]{0:T(128)S(1)}, s32[16]{0:T(128)}, u32[]{:S(2)}) copy-start(s32[16]{0:T(128)} %owners.3) | copy-start | bytes 196

commit v6 on v5

--- a/solution.py
+++ b/solution.py
@@ -74,6 +74,14 @@
     zm_other = (chip(y, z - 1, 1 - c), tp)
     far_other = chip(1 - y, z + 2, 1 - c)
 
+    barrier = pltpu.get_barrier_semaphore()
+
+    @pl.loop(0, REPS)
+    def _(k):
+        @pl.when((k != rep) & (k != COLLECTOR))
+        def _():
+            pl.semaphore_signal(barrier, inc=1, device_id=(k, tp), device_id_type=MESH)
+
     loads = [
         pltpu.make_async_copy(owners, own_s, load_sem.at[0]),
         pltpu.make_async_copy(hidden, hbuf, load_sem.at[1]),
@@ -88,14 +96,6 @@
     ]
     for load in loads[:5]:
         load.start()
-
-    barrier = pltpu.get_barrier_semaphore()
-
-    @pl.loop(0, REPS)
-    def _(k):
-        @pl.when((k != rep) & (k != COLLECTOR))
-        def _():
-            pl.semaphore_signal(barrier, inc=1, device_id=(k, tp), device_id_type=MESH)
 
     loads[1].wait()
     for r in range(REPS):
@@ -244,8 +244,10 @@
             p = jnp.exp(scores[s, :, pl.ds(start, CHUNK)] - top)
             for j in range(CHUNK // HEAD_DIM):
                 total = total + p[:, j * HEAD_DIM : (j + 1) * HEAD_DIM]
-            acc = acc + jnp.dot(p.astype(BF16), vbuf[s, pl.ds(start, CHUNK), :], preferred_element_type=F32)
-            return total, acc
+            high = p.astype(BF16)
+            both = jnp.concatenate([high, (p - high.astype(F32)).astype(BF16)], axis=0)
+            out = jnp.dot(both, vbuf[s, pl.ds(start, CHUNK), :], preferred_element_type=F32)
+            return total, acc + (out[:QROWS] + out[QROWS:])
 
         zero = jnp.zeros((QROWS, HEAD_DIM), F32)
         total, acc = lax.fori_loop(0, SLOTS // CHUNK, body, (zero, zero))
@@ -348,9 +350,9 @@
         def _(k):
             small(osend.at[part], orecv.at[part, tp], 2, (rep, lax.rem(tp + k, TPS))).start()
 
-    events(11, 12)
     events(17)
     events(7, 8)
+    events(11, 12)
     events(13, 14)
     events(9, 10)
     events(15, 16)

time: 28.7 us -> 28.7 us (level)
  no operation moved by 1% of the time
where the time goes in v6:
time: 28.7 us; the launch traced here: 28.6 us
  Pallas kernels  27.9 us (97%)
  between operations  0.66 us (2%)
    pallas_call x1, Pallas kernels, shards(): pl.pallas_call(main_kernel, out_shape=(pltpu.VMEM((REPS, ROWS, COLS), BF1...  25.2 us
    pallas_call x1, Pallas kernels, shards(): pl.pallas_call(write_kernel, out_shape=(jax.ShapeDtypeStruct((REPS, ROWS,...  2.7 us

profile of v6, /device:TPU:0, one launch (start us, length us, event | category | flops | bytes accessed | tf_op | source)
XLA Modules:
  0.0 28.6 jit_solution(9371809071289826808)
XLA Ops:
  0.6 0.0 copy-start
  0.6 25.2 %gather_and_attend.1 = (bf16[16,512,256]{2,1,0:T(8,128)(2,1)S(1)}, bf16[2,2,4096]{2,1,0:T(2,128)(2,1)S(1)}, bf16[2,2,256]{2,1,0:T(2,128)(2,1)S(1)}) custom-call(bf16[2,2,8192]{2,1,0:T(2,128)(2,1)} %hidden.1, bf16[2,2,1024]{2,1,0:T(2,128)(2,1)} %queries.1, bf16[512,256]{1,0:T(8,128)(2,1)} %sectioned.1, s32[16]{0:T(128)} %owners.3, ...), custom_call_target="tpu_custom_call" | custom-call | tf_op jit(solution)/shard_map/gather_and_attend/pallas_call | solution.py:403
  25.8 0.0 copy-done
  25.9 2.7 %write_in_order.1 = (bf16[16,512,256]{2,1,0:T(8,128)(2,1)}, bf16[2,2,4096]{2,1,0:T(2,128)(2,1)}, bf16[2,2,256]{2,1,0:T(2,128)(2,1)}) custom-call(s32[16]{0:T(128)S(1)} %copy-done, bf16[16,512,256]{2,1,0:T(8,128)(2,1)S(1)} %get-tuple-element.9.pooled, bf16[2,2,4096]{2,1,0:T(2,128)(2,1)S(1)} %get-tuple-element.10.attended, ...), custom_call_target="tpu_custom_call" | custom-call | tf_op jit(solution)/shard_map/write_in_order/pallas_call | solution.py:444
Async XLA Ops:
  0.6 25.2 %copy-start = (s32[16]{0:T(128)S(1)}, s32[16]{0:T(128)}, u32[]{:S(2)}) copy-start(s32[16]{0:T(128)} %owners.3) | copy-start | bytes 196

commit v7 on v6

--- a/solution.py
+++ b/solution.py
@@ -244,10 +244,8 @@
             p = jnp.exp(scores[s, :, pl.ds(start, CHUNK)] - top)
             for j in range(CHUNK // HEAD_DIM):
                 total = total + p[:, j * HEAD_DIM : (j + 1) * HEAD_DIM]
-            high = p.astype(BF16)
-            both = jnp.concatenate([high, (p - high.astype(F32)).astype(BF16)], axis=0)
-            out = jnp.dot(both, vbuf[s, pl.ds(start, CHUNK), :], preferred_element_type=F32)
-            return total, acc + (out[:QROWS] + out[QROWS:])
+            acc = acc + jnp.dot(p.astype(BF16), vbuf[s, pl.ds(start, CHUNK), :], preferred_element_type=F32)
+            return total, acc
 
         zero = jnp.zeros((QROWS, HEAD_DIM), F32)
         total, acc = lax.fori_loop(0, SLOTS // CHUNK, body, (zero, zero))

time: 28.7 us -> 28.7 us (level)
  no operation moved by 1% of the time
where the time goes in v7:
time: 28.7 us; the launch traced here: 28.6 us
  Pallas kernels  27.9 us (97%)
  between operations  0.66 us (2%)
    pallas_call x1, Pallas kernels, shards(): pl.pallas_call(main_kernel, out_shape=(pltpu.VMEM((REPS, ROWS, COLS), BF1...  25.2 us
    pallas_call x1, Pallas kernels, shards(): pl.pallas_call(write_kernel, out_shape=(jax.ShapeDtypeStruct((REPS, ROWS,...  2.7 us

profile of v7, /device:TPU:0, one launch (start us, length us, event | category | flops | bytes accessed | tf_op | source)
XLA Modules:
  0.0 28.6 jit_solution(2517029321113291043)
XLA Ops:
  0.6 0.0 copy-start
  0.6 25.2 %gather_and_attend.1 = (bf16[16,512,256]{2,1,0:T(8,128)(2,1)S(1)}, bf16[2,2,4096]{2,1,0:T(2,128)(2,1)S(1)}, bf16[2,2,256]{2,1,0:T(2,128)(2,1)S(1)}) custom-call(bf16[2,2,8192]{2,1,0:T(2,128)(2,1)} %hidden.1, bf16[2,2,1024]{2,1,0:T(2,128)(2,1)} %queries.1, bf16[512,256]{1,0:T(8,128)(2,1)} %sectioned.1, s32[16]{0:T(128)} %owners.3, ...), custom_call_target="tpu_custom_call" | custom-call | tf_op jit(solution)/shard_map/gather_and_attend/pallas_call | solution.py:401
  25.8 0.0 copy-done
  25.9 2.7 %write_in_order.1 = (bf16[16,512,256]{2,1,0:T(8,128)(2,1)}, bf16[2,2,4096]{2,1,0:T(2,128)(2,1)}, bf16[2,2,256]{2,1,0:T(2,128)(2,1)}) custom-call(s32[16]{0:T(128)S(1)} %copy-done, bf16[16,512,256]{2,1,0:T(8,128)(2,1)S(1)} %get-tuple-element.9.pooled, bf16[2,2,4096]{2,1,0:T(2,128)(2,1)S(1)} %get-tuple-element.10.attended, ...), custom_call_target="tpu_custom_call" | custom-call | tf_op jit(solution)/shard_map/write_in_order/pallas_call | solution.py:442
Async XLA Ops:
  0.6 25.2 %copy-start = (s32[16]{0:T(128)S(1)}, s32[16]{0:T(128)}, u32[]{:S(2)}) copy-start(s32[16]{0:T(128)} %owners.3) | copy-start | bytes 196
